TPU v7x, 32 devices: a whole 2x2x4 slice. The times are simulated.
32 devices in a mesh: stream: 2 (over x), batch: 16 (over z, y, core).
Axes of the slice: x: 2, y: 2, z: 4, core: 2. Of those that a mesh axis runs over, the one named last changes fastest.
Arguments:
- features: bfloat16 [2, 32, 512, 768], P('stream', 'batch'), may hold values from -6 to 6
- cotangent: bfloat16 [2, 32, 512, 768], P('stream', 'batch'), may hold values from -6 to 6
- segment_ids: int32 [32, 512], P('batch'), may hold values from 0 to 3, never falling along the last dimension, each value on 1 to 256 neighbouring positions
- box_cells: int32 [2, 32, 2, 512], P('stream', 'batch'), may hold values from 0 to 15
- ln_gain: float32 [2, 2, 768], P('stream'), may hold values from 0.5 to 1.5
- ln_shift: float32 [2, 2, 768], P('stream'), may hold values from -1.8 to 1.8
- w_qkv: bfloat16 [2, 768, 2304], P('stream'), may hold values from -0.21875 to 0.21875
- attn_bias: float32 [2, 3, 768], P('stream'), may hold values from -1.8 to 1.8
- distance_table: float32 [2, 64, 12], P('stream'), may hold values from -4 to 4
- w_out: bfloat16 [2, 768, 768], P('stream'), may hold values from -1.25 to 1.25
- w_up: bfloat16 [2, 768, 3072], P('stream'), may hold values from -0.21875 to 0.21875
- up_bias: float32 [2, 3072], P('stream'), may hold values from -1.8 to 1.8
- w_down: bfloat16 [2, 3072, 768], P('stream'), may hold values from -0.109375 to 0.109375
- down_bias: float32 [2, 768], P('stream'), may hold values from -1.8 to 1.8
Outputs:
- output: bfloat16 [2, 32, 512, 768], P('stream', 'batch')
- input_grad: bfloat16 [2, 32, 512, 768], P('stream', 'batch')
- grad_ln_gain: float32 [2, 2, 768], P('stream')
- grad_ln_shift: float32 [2, 2, 768], P('stream')
- grad_w_qkv: float32 [2, 768, 2304], P('stream')
- grad_attn_bias: float32 [2, 3, 768], P('stream')
- grad_distance_table: float32 [2, 64, 12], P('stream')
- grad_w_out: float32 [2, 768, 768], P('stream')
- grad_w_up: float32 [2, 768, 3072], P('stream')
- grad_up_bias: float32 [2, 3072], P('stream')
- grad_w_down: float32 [2, 3072, 768], P('stream')
- grad_down_bias: float32 [2, 768], P('stream')
Inputs may be any that keep to these rules, and one draw needn't show every extreme that they name: `segment_ids`: along each row the document numbers never fall; every document has 1 to 256 tokens and one has 256.
All inputs are finite; a program needn't handle non-finite values.
Results may differ from a plain program's by a relative error of at most 0.015.
Values may be sent and summed in bfloat16 or wider, within the bound.
A program may use at most 320 MiB of HBM per device.

v0:
```python
import functools
import jax
import jax.numpy as jnp
from jax import lax
from jax.experimental import pallas as pl
from jax.experimental.pallas import tpu as pltpu
from jax.sharding import PartitionSpec as P

GRID = 8
EPSILON = 1e-05
MASKED = -1000000000.0

NT=(((1,),(1,)),((),())); NN=(((1,),(0,)),((),())); TN=(((0,),(0,)),((),()))
def mm(a,b,dn=NN): return lax.dot_general(a,b,dn,preferred_element_type=jnp.float32)
BF=jnp.bfloat16

def three(x):
    hi=x.astype(BF); r=x-hi.astype(jnp.float32); mid=r.astype(BF); lo=(r-mid.astype(jnp.float32)).astype(BF)
    return hi,mid,lo

def fwd_kernel(CQ, q_ref,kn_ref,kf_ref,vn_ref,vf_ref,e_ref,b_ref,qseg_ref,kseg_ref,o_ref,qm_ref):
    pair=pl.program_id(1)
    L=q_ref.shape[0]
    lane=lax.broadcasted_iota(jnp.int32,(1,128),1)
    @pl.when(pair==0)
    def _():
        qm_ref[...]=qseg_ref[...]
    outs=[None]*(L//CQ)
    for hh in range(2):
        mh=(lane<64) if hh==0 else (lane>=64)
        h=2*pair+hh
        C=mm(e_ref[...],b_ref[hh]).astype(BF)
        kx=jnp.concatenate([kn_ref[...],C,kseg_ref[...]],axis=1)
        kf=kf_ref[...]
        one=jnp.ones((),BF); zero=jnp.zeros((),BF)
        vnx=jnp.where(mh,vn_ref[...],one); vfx=jnp.where(mh,vf_ref[...],one)
        for c in range(L//CQ):
            sl=slice(c*CQ,(c+1)*CQ)
            qm=jnp.where(mh,q_ref[sl,:],zero)
            qx=jnp.concatenate([qm,e_ref[sl,:],qseg_ref[sl,:]],axis=1)
            sn=mm(qx,kx,NT); sf=mm(qm,kf,NT)
            m=jnp.maximum(jnp.max(sn,axis=1,keepdims=True),jnp.max(sf,axis=1,keepdims=True))
            pn=jnp.exp(sn-m).astype(BF); pf=jnp.exp(sf-m).astype(BF)
            o=mm(pn,vnx)+mm(pf,vfx)
            l=pltpu.roll(o,64,1)
            on=o/l
            outs[c]=on if hh==0 else jnp.where(mh,on,outs[c])
            lse=-(m+jnp.log(jnp.where(mh,l,o)))
            hi,mid,lo=three(lse)
            cur=qm_ref[sl,:]
            cur=jnp.where(lane==3*h,hi,cur); cur=jnp.where(lane==3*h+1,mid,cur); cur=jnp.where(lane==3*h+2,lo,cur)
            qm_ref[sl,:]=cur
    for c in range(L//CQ):
        o_ref[c*CQ:(c+1)*CQ,:]=outs[c].astype(BF)

def fwd(q,kn,kf,vn,vf,e,bt,qseg,kseg,L,CQ=512):
    T=q.shape[0]; R=T//L; NP=q.shape[1]//128
    blk=pl.BlockSpec((L,128),lambda r,p:(r,p))
    row=lambda w: pl.BlockSpec((L,w),lambda r,p:(r,0))
    return pl.pallas_call(functools.partial(fwd_kernel,CQ),grid=(R,NP),
        in_specs=[blk]*5+[row(256),pl.BlockSpec((2,256,256),lambda r,p:(p,0,0)),row(128),row(128)],
        out_specs=[blk,row(128)],
        out_shape=[jax.ShapeDtypeStruct(q.shape,BF),jax.ShapeDtypeStruct((T,128),BF)],
        compiler_params=pltpu.CompilerParams(vmem_limit_bytes=48<<20),name="att_fwd")(q,kn,kf,vn,vf,e,bt,qseg,kseg)


F32=jnp.float32


MESH=pl.DeviceIdType.MESH
SIDE=768
WIDE=384
LAG=3
STEP=48

def bit_order(n, c):
    plain=list(range(n.bit_length()-1))
    other=[0]+plain[2:]+[1] if len(plain)>2 else plain
    return other if c%6==3 else plain

def plan_of(bits, rows):
    sizes=[rows]
    for _ in range(bits):
        m=sizes[-1]
        sizes.append(m//2 if m%32==0 else m)
    return sizes

def place(me, b):
    bit=(me//(1<<b))%2
    return bit, me+(1-2*bit)*(1<<b)

def rows_at(off, size):
    return pl.ds(off if isinstance(off,int) else pl.multiple_of(off,16),size)

class Engine:
    def __init__(self, n, me, lag, chunks, x, recv, segs, sums, ss, rs, os):
        self.me,self.lag,self.chunks=me,lag,chunks
        self.x,self.recv,self.segs,self.sums=x,recv,segs,sums
        self.ss,self.rs,self.os=ss,rs,os
        self.bits=n.bit_length()-1
        self.sizes=plan_of(self.bits,SIDE)
        self.offs=[sum(self.sizes[1:s+1]) for s in range(self.bits+1)]
        self.n=n

    def seg(self,c,upto):
        order=bit_order(self.n,self.chunks[c]["kind"]); off=0
        for s in range(upto):
            if self.sizes[s+1]!=self.sizes[s]:
                off=off+place(self.me,order[s])[0]*self.sizes[s+1]
        return off,self.sizes[upto]

    def out(self,c,off,m):
        a,i,k=self.chunks[c]["to"]
        return self.sums[a].at[rows_at(i*SIDE+off,m),pl.ds(k*WIDE,WIDE)]

    def final(self,c):
        off,m=self.seg(c,self.bits)
        ch=self.chunks[c]
        if ch["first"]: return self.segs.at[ch["seg"]]
        return self.x.at[ch["slot"],rows_at(off,m)]

    def copy(self,c,stage):
        B,sizes,ch=self.bits,self.sizes,self.chunks[c]
        order=bit_order(self.n,ch["kind"])
        if stage<B:
            bit,partner=place(self.me,order[stage])
            off,m=self.seg(c,stage)
            if sizes[stage+1]!=m:
                src=self.x.at[ch["slot"],rows_at(off+(1-bit)*(m//2),m//2)]
            else:
                src=self.x.at[ch["slot"],rows_at(off,m)]
            dst=self.recv.at[ch["land"],pl.ds(self.offs[stage],sizes[stage+1])]
        else:
            s=2*B-1-stage
            if sizes[s+1]==sizes[s]:
                return None
            partner=place(self.me,order[s])[1]
            off,m=self.seg(c,s+1)
            dst=self.out(c,off,m)
            src=self.final(c) if stage==B else dst
        return pltpu.make_async_remote_copy(src,dst,self.ss.at[c,stage],self.rs.at[c,stage],
            device_id={"batch":partner},device_id_type=MESH)

    def keep(self,c):
        off,m=self.seg(c,self.bits)
        return pltpu.make_async_copy(self.final(c),self.out(c,off,m),self.os.at[c])

    def start(self,c,stage):
        if stage==self.bits:
            self.keep(c).start()
        d=self.copy(c,stage)
        if d is not None: d.start()

    def finish(self,c,stage):
        d=self.copy(c,stage)
        if d is not None: d.wait()
        if stage==self.bits:
            self.keep(c).wait()
        if stage<self.bits:
            off,m=self.seg(c,stage+1)
            ro=self.offs[stage]; x,recv=self.x,self.recv
            h,land=self.chunks[c]["slot"],self.chunks[c]["land"]
            def body(i,_):
                at=rows_at(off+i*STEP,STEP)
                more=recv[land,pl.ds(pl.multiple_of(ro+i*STEP,16),STEP)]
                x[h,at]=(x[h,at].astype(F32)+more.astype(F32)).astype(BF)
                return 0
            lax.fori_loop(0,m//STEP,body,0)
            if stage==self.bits-1 and self.chunks[c]["last"]==self.bits:
                self.segs[self.chunks[c]["seg"]]=x[h,rows_at(off,m)]

    def slot(self,t,load):
        for c in sorted(range(len(self.chunks)),key=lambda c:self.chunks[c]["entry"]):
            ch=self.chunks[c]
            if t<ch["entry"] or (t-ch["entry"])%self.lag: continue
            s=ch["first"]+(t-ch["entry"])//self.lag
            if s>ch["last"]: continue
            if s==ch["first"]: load(c)
            else: self.finish(c,s-1)
            if s<ch["last"]: self.start(c,s)

    def end(self):
        return 1+max(ch["entry"]+self.lag*(ch["last"]-ch["first"]) for ch in self.chunks)

def small_copy(me,x,recv,ss,rs,s):
    return pltpu.make_async_remote_copy(x.at[s],recv.at[s],ss.at[s],rs.at[s],device_id={"batch":place(me,s)[1]},device_id_type=MESH)

def back_kernel(n, NP, R, chunks, loads, cuts,
               q_ref,kn_ref,kf_ref,vn_ref,vf_ref,do_ref,dm_ref,qm_ref,e_ref,et_ref,b_ref,kseg_ref,qf_ref,qmf_ref,
               feat_ref,wqkv_ref,gm_ref,vec_ref,early_ref,
               do_any,dm_any,segs,gu_any,gd_any,go_any,
               ig_ref,smalla_ref,smallb_ref,su_any,sd_any,so_any,sq_any,
               dof,dmf,gmix,nt_s,g_s,tab,x,recv,ax,arecv,bx,brecv,in_sem,out_sem,ss,rs,xs_sem,xr_sem,a_ss,a_rs,b_ss,b_rs):
    step=pl.program_id(0)
    per=NP*R
    second=(step>=per)&(step<2*per)
    inner=step%per; pair=inner//R; r=inner%R
    L=q_ref.shape[0]; T=feat_ref.shape[0]; D=feat_ref.shape[1]
    me=lax.axis_index("batch"); other={"stream":1-lax.axis_index("stream")}
    lane=lax.broadcasted_iota(jnp.int32,(1,128),1)
    zero=jnp.zeros((),BF)
    RC=256
    grads=(gu_any,gd_any,go_any)
    eng=Engine(n,me,LAG,chunks,x,recv,segs,(su_any,sd_any,so_any,sq_any),ss,rs,out_sem)
    B=eng.bits
    q_set,mid_set,end_set=[[c for c in range(len(chunks)) if chunks[c].get("set")==i] for i in range(3)]
    def load(c):
        a,k=loads[c]
        return pltpu.make_async_copy(grads[a].at[:,pl.ds(k*WIDE,WIDE)],x.at[chunks[c]["slot"]],in_sem.at[c])
    def ready(c):
        if c in loads: load(c).wait()
    def across():
        res=[pltpu.make_async_remote_copy(dm_any,dmf,xs_sem.at[NP],xr_sem.at[NP],device_id=other,device_id_type=MESH)]
        for p in range(NP):
            res.append(pltpu.make_async_remote_copy(do_any.at[:,pl.ds(p*128,128)],dof.at[p],xs_sem.at[p],xr_sem.at[p],device_id=other,device_id_type=MESH))
        return res

    @pl.when(step==0)
    def _():
        sem=pltpu.get_barrier_semaphore()
        for b in range(B):
            pl.semaphore_signal(sem,inc=1,device_id={"batch":place(me,b)[1]},device_id_type=MESH)
        pl.semaphore_signal(sem,inc=1,device_id=other,device_id_type=MESH)
        for c in loads: load(c).start()
        pl.semaphore_wait(sem,B+1)
        for d in across(): d.start()
    def spread(lo,hi,parts): return [lo+(hi-lo)*i//parts for i in range(parts)]
    edges=spread(0,cuts[0],2*per)+spread(cuts[0],cuts[1],per)+spread(cuts[1],cuts[2],per)+[cuts[2]]
    def form(c):
        a,i,k=chunks[c]["to"]
        x[chunks[c]["slot"]]=mm(nt_s[i*SIDE:(i+1)*SIDE,:],gmix[:,k*WIDE:(k+1)*WIDE]).astype(BF)
    def tick(half):
        for k in range(2*per):
            i=k*2+half
            small_now=half==0 and k>=per and k-per<=B
            group=q_set if i==2*per else mid_set if i==3*per else []
            if edges[i]==edges[i+1] and not small_now and not group: continue
            @pl.when(step==k)
            def _():
                if i==2*per:
                    for j in range(T//RC):
                        sl=slice(j*RC,(j+1)*RC)
                        nrm,_=norm_parts(feat_ref[sl,:].astype(F32))
                        nt_s[:,sl]=(nrm*vec_ref[0:1,:]+vec_ref[1:2,:]).astype(BF).T
                for c in group: form(c)
                for t in range(edges[i],edges[i+1]): eng.slot(t,ready)
                if small_now:
                    s=k-per
                    if s==0:
                        put=(lax.broadcasted_iota(jnp.int32,(256,128),1)==lax.broadcasted_iota(jnp.int32,(256,128),0)//16).astype(BF)
                        ax[0,:2*NP*16]=sum(mm(v,put) for v in three(tab[...]))
                        ax[0,2*NP*16:]=early_ref[...]
                    else:
                        small_copy(me,ax,arecv,a_ss,a_rs,s-1).wait()
                        ax[s]=ax[s-1]+arecv[s-1]
                    if s<B: small_copy(me,ax,arecv,a_ss,a_rs,s).start()
                    else: smalla_ref[...]=ax[B]
    def half_of(hh):
        return (lane<64) if hh==0 else (lane>=64)
    def ones_of(h):
        return jnp.where((lane>=3*h)&(lane<3*h+3),1.0,0.0)
    add=lambda a,b: b if a is None else a+b
    def cols(part): return pl.ds(pl.multiple_of(part*D+pair*128,128),128)
    at=pl.ds(pl.multiple_of(r*L,L),L)

    tick(0)
    @pl.when(step<per)
    def _():
        dkn=None; dvn=None; dq=None
        for hh in range(2):
            mh=half_of(hh); h=2*pair+hh
            ones_h=ones_of(h); ones_b=jnp.broadcast_to(ones_h.astype(BF),(L,128))
            qm=jnp.where(mh,q_ref[...],zero); dom=jnp.where(mh,do_ref[...],zero)
            C_h=mm(e_ref[...],b_ref[hh]).astype(BF)
            qx=jnp.concatenate([qm,e_ref[...],qm_ref[...]],axis=1)
            dox=jnp.concatenate([dom,dm_ref[...]],axis=1)
            kseg=(kseg_ref[...].astype(F32)+ones_h).astype(BF)
            p=jnp.exp(mm(jnp.concatenate([kn_ref[...],C_h,kseg],axis=1),qx,NT))
            ds=(p*mm(jnp.concatenate([vn_ref[...],ones_b],axis=1),dox,NT)).astype(BF)
            dvn=add(dvn,mm(p.astype(BF),dom))
            t=mm(ds,jnp.concatenate([qm,e_ref[...]],axis=1))
            dkn=add(dkn,t[:,:128])
            g=mm(et_ref[...],t[:,128:].astype(BF))
            dq=add(dq,mm(ds,jnp.where(mh,kn_ref[...],zero),TN))
            p=jnp.exp(mm(jnp.concatenate([kf_ref[...],ones_b],axis=1),jnp.concatenate([qm,qm_ref[...]],axis=1),NT))
            ds=(p*mm(jnp.concatenate([vf_ref[...],ones_b],axis=1),dox,NT)).astype(BF)
            dq=add(dq,mm(ds,jnp.where(mh,kf_ref[...],zero),TN))
            @pl.when(r==0)
            def _(): g_s[hh]=g
            @pl.when(r!=0)
            def _(): g_s[hh]+=g
        gmix[at,cols(0)]=(dq*0.125).astype(BF)
        gmix[at,cols(1)]=dkn.astype(BF); gmix[at,cols(2)]=dvn.astype(BF)
    @pl.when((step<per)&(r==R-1))
    def _():
        turn=lax.broadcasted_iota(jnp.int32,(1,256),1)
        gap=jnp.minimum(jnp.abs(lax.broadcasted_iota(jnp.int32,(16,256),0)-turn%16),7)
        for hh in range(2):
            ahead=None; behind=None
            for i in range(16):
                blk=g_s[hh,16*i:16*i+16,:]
                if i: blk=pltpu.roll(blk,256-16*i,1)
                ahead=add(ahead,jnp.where(turn<256-16*i,blk,0.0))
                behind=add(behind,jnp.where(turn<256-16*i,0.0,blk))
            sums=[colsum(jnp.where(gap==k,v,0.0)) for v in (ahead,behind) for k in range(8)]
            tab[pl.ds(pl.multiple_of((2*pair+hh)*16,16),16),:]=jnp.concatenate(sums,axis=0)
    tick(1)
    @pl.when(step==per)
    def _():
        for d in across(): d.wait_recv()
    @pl.when(second)
    def _():
        dk=gmix[at,cols(1)].astype(F32); dv=gmix[at,cols(2)].astype(F32)
        for hh in range(2):
            mh=half_of(hh); h=2*pair+hh
            ones_b=jnp.broadcast_to(ones_of(h).astype(BF),(L,128))
            qm=jnp.where(mh,qf_ref[...],zero); dom=jnp.where(mh,dof[pair,at],zero)
            p=jnp.exp(mm(jnp.concatenate([kn_ref[...],ones_b],axis=1),jnp.concatenate([qm,qmf_ref[...]],axis=1),NT))
            ds=(p*mm(jnp.concatenate([vn_ref[...],ones_b],axis=1),jnp.concatenate([dom,dmf[at]],axis=1),NT)).astype(BF)
            dv=dv+mm(p.astype(BF),dom)
            dk=dk+mm(ds,qm)
        gmix[at,cols(1)]=dk.astype(BF); gmix[at,cols(2)]=dv.astype(BF)
    @pl.when(step==2*per)
    def _():
        now=cuts[2]
        for c in end_set:
            form(c); eng.slot(now,ready); now+=1
        gain=0.0; shift=0.0; qb=0.0; vb=0.0
        for i in range(T//RC):
            sl=slice(i*RC,(i+1)*RC)
            g=mm(gmix[sl,:],wqkv_ref[...],NT)
            nrm,inv=norm_parts(feat_ref[sl,:].astype(F32))
            gain=gain+colsum(g*nrm); shift=shift+colsum(g)
            qb=qb+colsum(gmix[sl,:D].astype(F32)); vb=vb+colsum(gmix[sl,2*D:].astype(F32))
            qg=g*vec_ref[0:1,:]
            ig_ref[sl,:]=(gm_ref[sl,:]+(qg-jnp.mean(qg,axis=1,keepdims=True)-nrm*jnp.mean(qg*nrm,axis=1,keepdims=True))*inv).astype(BF)
            eng.slot(now,ready); now+=1
        w=D//128
        for i,v in enumerate((gain,shift,qb,vb)):
            for k in range(w): bx[0,i*w+k:i*w+k+1,:]=v[:,k*128:(k+1)*128]
        small_copy(me,bx,brecv,b_ss,b_rs,0).start()
        done=1
        for t in range(now,max(eng.end(),now+LAG*B)):
            eng.slot(t,ready)
            if (t-now)%LAG==LAG-1 and done<=B:
                small_copy(me,bx,brecv,b_ss,b_rs,done-1).wait()
                bx[done]=bx[done-1]+brecv[done-1]
                if done<B: small_copy(me,bx,brecv,b_ss,b_rs,done).start()
                done+=1
        assert done==B+1
        smallb_ref[...]=bx[B]
        for d in across(): d.wait_send()

def back(q,kn,kf,vn,vf,do,dm,qmisc,e,et,bt,kseg,qf,qmf,feat,wqkv,gm,vec,early,segs,grads,full_ff,L,n,collective_id):
    T,D=q.shape; R=T//L; NP=D//128; per=R*NP
    def one(step): i=jnp.minimum(step,per-1); return i%R,i//R
    def cyc(step): i=jnp.minimum(step,2*per-1)%per; return i%R,i//R
    def two(step): i=jnp.clip(step-per,0,per-1); return i%R,i//R
    blk=lambda f: pl.BlockSpec((L,128),f)
    row=lambda w,f: pl.BlockSpec((L,w),lambda s:(f(s)[0],0))
    full=lambda a: pl.BlockSpec(a.shape,lambda s:(0,)*len(a.shape),pipeline_mode=pl.Buffered(1))
    any_=pl.BlockSpec(memory_space=pl.ANY)
    S=jax.ShapeDtypeStruct; sem=pltpu.SemaphoreType.DMA
    bits=n.bit_length()-1; per_side=D//WIDE; tiles=full_ff//SIDE
    first=max(20,LAG*(bits+1)+per_side)
    cuts=(first,first+9,first+20)
    chunks=[]; loads={}
    def chunk(to,entry,**more):
        ch=dict(to=to,entry=entry,kind=len(chunks),first=0,last=2*bits); ch.update(more); chunks.append(ch)
    for i,(a,r,k) in enumerate([(0,0,(tiles-1)*per_side+k) for k in range(per_side)]+[(1,tiles-1,k) for k in range(per_side)]+[(2,0,k) for k in range(per_side)]):
        loads[len(chunks)]=(a,i%per_side)
        chunk((a,r,k),3*i,slot=i,land=i)
    place_of=[p for t in range(tiles-1) for p in [(0,0,t*per_side+k) for k in range(per_side)]+[(1,t,k) for k in range(per_side)]]
    spare=[t for t in range(first) if t%3 or t>=3*len(loads)]
    for i,p in enumerate(place_of):
        chunk(p,spare[i],first=bits,seg=i,kind=i)
    at=len(loads)
    half=per_side//2
    for g,group in enumerate(([k for k in range(per_side)],[per_side+k for k in range(half)]+[2*per_side+k for k in range(half)],
                  [per_side+k for k in range(half,per_side)]+[2*per_side+k for k in range(half,per_side)])):
        for i,k in enumerate(group):
            chunk((3,0,k),cuts[g]+i,slot=at,land=at,set=g); at+=1
    C=len(chunks)
    rows=sum(plan_of(bits,SIDE)[1:])
    asmall=(2*NP*16+early.shape[0],128); bsmall=(4*D//128,128)
    outs=[S((T,D),BF),S(asmall,F32),S(bsmall,F32)]
    sums=[S((D,full_ff),BF),S((full_ff,D),BF),S((D,D),BF),S(wqkv.shape,BF)]
    return pl.pallas_call(functools.partial(back_kernel,n,NP,R,chunks,loads,cuts),grid=(2*per+1,),
        in_specs=[blk(one),blk(cyc),blk(one),blk(cyc),blk(one),blk(one),row(128,one),row(128,one),row(256,one),
                  pl.BlockSpec((256,L),lambda s:(0,one(s)[0])),pl.BlockSpec((2,256,256),lambda s:(one(s)[1],0,0)),row(128,one),blk(two),row(128,two),
                  full(feat),full(wqkv),full(gm),full(vec),full(early)]+[any_]*2+[full(segs)]+[any_]*3,
        out_specs=[full(o) for o in outs]+[any_]*4,
        out_shape=outs+sums,
        scratch_shapes=[pltpu.VMEM((NP,T,128),BF),pltpu.VMEM((T,128),BF),pltpu.VMEM((T,3*D),BF),pltpu.VMEM((D,T),BF),pltpu.VMEM((2,256,256),F32),pltpu.VMEM((2*NP*16,256),F32),
            pltpu.VMEM((at,SIDE,WIDE),BF),pltpu.VMEM((at,rows,WIDE),BF),
            pltpu.VMEM((bits+1,)+asmall,F32),pltpu.VMEM((bits,)+asmall,F32),pltpu.VMEM((bits+1,)+bsmall,F32),pltpu.VMEM((bits,)+bsmall,F32),
            sem((C,)),sem((C,)),sem((C,2*bits)),sem((C,2*bits)),sem((NP+1,)),sem((NP+1,)),sem((bits,)),sem((bits,)),sem((bits,)),sem((bits,))],
        compiler_params=pltpu.CompilerParams(collective_id=collective_id,has_side_effects=True,vmem_limit_bytes=64<<20),
        name="att_bwd")(q,kn,kf,vn,vf,do,dm,qmisc,e,et,bt,kseg,qf,qmf,feat,wqkv,gm,vec,early,do,dm,segs,*grads)


def gelu_both(u):
    a=jnp.abs(u)
    t=1.0/(1.0+a*(0.3275911*0.7071067811865476))
    ex=jnp.exp(u*u*-0.5)
    poly=((((1.061405429*t-1.453152027)*t+1.421413741)*t-0.284496736)*t+0.254829592)*t
    half=0.5*poly*ex
    cdf=jnp.where(u<0,half,1.0-half)
    return u*cdf, cdf+u*ex*0.3989422804014327

def norm_parts(v):
    center=v-jnp.mean(v,axis=1,keepdims=True)
    inv=lax.rsqrt(jnp.mean(center*center,axis=1,keepdims=True)+EPSILON)
    return center*inv,inv

def colsum(v): return jnp.sum(v,axis=0,keepdims=True)


MID_LAG=2
def mid_kernel(n, chunks, TILES, x_ref,cot_ref,att_ref,wo_ref,vec_ref,wu_ref,wd_ref,ub_ref,
               out_ref,gm_ref,do_ref,dm_ref,gwo_ref,gul_ref,gdl_ref,gub_ref,small_ref,seg_ref,
               mid_s,nt_s,ntt_s,acc_s,gn_s,act_s,gp_s,x,recv,ss,rs):
    j=pl.program_id(0); T=x_ref.shape[0]; D=x_ref.shape[1]; RC=256
    parts=[slice(i*RC,(i+1)*RC) for i in range(T//RC)]
    me=lax.axis_index("batch")
    eng=Engine(n,me,MID_LAG,chunks,x,recv,seg_ref,None,ss,rs,None)
    per_tile=2*D//WIDE; pace=2*len(parts)
    def tick(i):
        for jj in range(1,TILES):
            @pl.when(j==jj)
            def _():
                for t in range(2*i,2*i+2): eng.slot(pace*(jj-1)+t,lambda c:None)
    @pl.when(j==0)
    def _():
        sem=pltpu.get_barrier_semaphore()
        for b in range(eng.bits):
            pl.semaphore_signal(sem,inc=1,device_id={"batch":place(me,b)[1]},device_id_type=MESH)
        for sl in parts:
            v=x_ref[sl,:].astype(F32)+mm(att_ref[sl,:],wo_ref[...])+vec_ref[0:1,:]
            mid_s[sl,:]=v
            nrm,_=norm_parts(v)
            nt=(nrm*vec_ref[1:2,:]+vec_ref[2:3,:]).astype(BF)
            nt_s[sl,:]=nt
            ntt_s[:,sl]=nt.T
            acc_s[sl,:]=v+vec_ref[3:4,:]
            gn_s[sl,:]=jnp.zeros_like(v)
        pl.semaphore_wait(sem,eng.bits)
    gub=0.0
    for i,sl in enumerate(parts):
        tick(i)
        pre=mm(nt_s[sl,:],wu_ref[...])+ub_ref[...]
        act,slope=gelu_both(pre)
        act=act.astype(BF)
        gp=(mm(cot_ref[sl,:],wd_ref[...],NT)*slope).astype(BF)
        act_s[sl,:]=act; gp_s[sl,:]=gp
        acc_s[sl,:]+=mm(act,wd_ref[...])
        gn_s[sl,:]+=mm(gp,wu_ref[...],NT)
        gub=gub+colsum(gp.astype(F32))
    gub_ref[...]=gub
    for k in range(D//WIDE):
        cs=slice(k*WIDE,(k+1)*WIDE)
        up=mm(ntt_s[...],gp_s[:,cs]).astype(BF)
        down=mm(act_s[...],cot_ref[:,cs],TN).astype(BF)
        @pl.when(j<TILES-1)
        def _():
            x[per_tile*j+k]=up
            x[per_tile*j+D//WIDE+k]=down
        @pl.when(j==TILES-1)
        def _():
            gul_ref[:,cs]=up; gdl_ref[:,cs]=down
    @pl.when(j==TILES-1)
    def _():
        g2=0.0; s2=0.0; ob=0.0; db=0.0; gwo=0.0
        row=lax.broadcasted_iota(jnp.int32,(D,128),0)//64
        col=lax.broadcasted_iota(jnp.int32,(D,128),1)
        pick=(row==col//3).astype(BF)
        lane=lax.broadcasted_iota(jnp.int32,(1,128),1)
        now=pace*(TILES-1)
        for sl in parts:
            out_ref[sl,:]=acc_s[sl,:].astype(BF)
            nrm,inv=norm_parts(mid_s[sl,:])
            q=gn_s[sl,:]
            g2=g2+colsum(q*nrm); s2=s2+colsum(q)
            qg=q*vec_ref[1:2,:]
            cot=cot_ref[sl,:].astype(F32)
            db=db+colsum(cot)
            gm=cot+(qg-jnp.mean(qg,axis=1,keepdims=True)-nrm*jnp.mean(qg*nrm,axis=1,keepdims=True))*inv
            gm_ref[sl,:]=gm
            gb=gm.astype(BF)
            gp_s[sl,:]=gb
            ob=ob+colsum(gb.astype(F32))
            do=mm(gb,wo_ref[...],NT).astype(BF)
            do_ref[sl,:]=do
            prod=do.astype(F32)*att_ref[sl,:].astype(F32)
            hi=prod.astype(BF); lo=(prod-hi.astype(F32)).astype(BF)
            delta=-(mm(hi,pick)+mm(lo,pick))
            hi,md,lo=three(delta)
            dm_ref[sl,:]=jnp.where(lane>=6*(D//128),jnp.zeros((),BF),jnp.where(lane%3==0,hi,jnp.where(lane%3==1,md,lo)))
            eng.slot(now,lambda c:None); now+=1
        gwo_ref[...]=mm(att_ref[...],gp_s[...],TN).astype(BF)
        small_ref[0:1,:]=g2; small_ref[1:2,:]=s2; small_ref[2:3,:]=ob; small_ref[3:4,:]=db
        small_ref[4:8,:]=jnp.zeros((4,D),F32)
        for t in range(now,eng.end()): eng.slot(t,lambda c:None)

def mid(x,cot,att,wo,vec,wu,wd,ub,n,collective_id):
    T,D=x.shape; FF=wu.shape[1]; FT=SIDE; TILES=FF//FT
    bits=n.bit_length()-1; pace=2*(T//256); per_tile=2*D//WIDE
    sizes=plan_of(bits,SIDE)
    chunks=[dict(entry=pace*(c//per_tile)+c%per_tile,kind=c,first=0,last=bits,slot=c,land=c,seg=c) for c in range(per_tile*(TILES-1))]
    C=len(chunks)
    one=lambda a: pl.BlockSpec(a.shape,lambda j:(0,)*len(a.shape),pipeline_mode=pl.Buffered(1))
    S=jax.ShapeDtypeStruct; sem=pltpu.SemaphoreType.DMA
    outs=[S((T,D),BF),S((T,D),F32),S((T,D),BF),S((T,128),BF),S((D,D),BF),S((D,D),BF),S((D,D),BF)]
    tail=[S((8,D),F32),S((C,sizes[-1],WIDE),BF)]
    return pl.pallas_call(functools.partial(mid_kernel,n,chunks,TILES),grid=(TILES,),
        in_specs=[one(x),one(cot),one(att),one(wo),one(vec),pl.BlockSpec((D,FT),lambda j:(0,j)),pl.BlockSpec((FT,D),lambda j:(j,0)),pl.BlockSpec((1,FT),lambda j:(0,j))],
        out_specs=[one(o) for o in outs]+[pl.BlockSpec((1,FT),lambda j:(0,j))]+[one(o) for o in tail],
        out_shape=outs+[S((1,FF),F32)]+tail,
        scratch_shapes=[pltpu.VMEM((T,D),F32),pltpu.VMEM((T,D),BF),pltpu.VMEM((D,T),BF),pltpu.VMEM((T,D),F32),pltpu.VMEM((T,D),F32),
            pltpu.VMEM((T,FT),BF),pltpu.VMEM((T,FT),BF),
            pltpu.VMEM((C,SIDE,WIDE),BF),pltpu.VMEM((C,sum(sizes[1:]),WIDE),BF),sem((C,bits)),sem((C,bits))],
        compiler_params=pltpu.CompilerParams(collective_id=collective_id,has_side_effects=True,vmem_limit_bytes=64<<20),name="feed_forward")(x,cot,att,wo,vec,wu,wd,ub)


def from_partner(block, axis, stride):
    count = lax.axis_size(axis)
    route = []
    for low in range(count):
        high = low | 1 << stride
        if high != low and high < count:
            route += [(low, high), (high, low)]
    return lax.ppermute(block, axis, route)


def layer_norm(values, norm_gain, norm_shift):
    center = values - jnp.mean(values, axis=-1, keepdims=True)
    spread = jnp.mean(center * center, axis=-1, keepdims=True)
    return center * lax.rsqrt(spread + EPSILON) * norm_gain + norm_shift


def norm_back(values, norm_gain, norm_shift, upstream):
    unused, pull_back = jax.vjp(layer_norm, values, norm_gain, norm_shift)
    return pull_back(upstream)


def gelu_exact(values):
    return jax.nn.gelu(values, approximate=False)


def gelu_back(values, upstream):
    unused, pull_back = jax.vjp(gelu_exact, values)
    return pull_back(upstream)[0]


def prepare(segment_ids, box_cells, table, is_vision):
    cell = (box_cells[:, 0] * 16 + box_cells[:, 1]).reshape(-1)
    cells = jnp.arange(256)
    e = (cell[:, None] == cells[None]).astype(BF)
    et = (cells[:, None] == cell[None]).astype(BF)
    lane = jnp.arange(128)
    same = segment_ids.reshape(-1)[:, None] == lane[None] - 64
    inside = (lane >= 64) & (lane < 68)
    qseg = same.astype(BF)
    kseg = jnp.where(inside[None] & ~same & jnp.logical_not(is_vision), MASKED, 0.0).astype(BF)
    return e, et, qseg, kseg


def code_onehot():
    c = jnp.arange(65536)
    step_x = jnp.minimum(jnp.abs(c // 4096 - (c // 16) % 16), GRID - 1)
    step_y = jnp.minimum(jnp.abs((c // 256) % 16 - c % 16), GRID - 1)
    return ((step_x * GRID + step_y)[None] == jnp.arange(GRID * GRID)[:, None]).astype(BF)


def on_device(features, cotangent, segment_ids, box_cells, ln_gain, ln_shift, w_qkv, attn_bias,
              distance_table, w_out, w_up, up_bias, w_down, down_bias):
    rows, length, width = features.shape[1:]
    tokens = rows * length
    heads = distance_table.shape[2]
    is_vision = lax.axis_index("stream") != 0
    norm_gains, norm_shifts = ln_gain[0], ln_shift[0]
    bias_rows = attn_bias[0]
    qkv_weight, out_weight, up_weight, down_weight = w_qkv[0], w_out[0], w_up[0], w_down[0]
    plain_in = features[0].reshape(tokens, width).astype(jnp.float32)
    normed = layer_norm(plain_in, norm_gains[0], norm_shifts[0]).astype(BF)
    combined = jnp.dot(normed, qkv_weight, preferred_element_type=jnp.float32)
    queries = (combined[:, :width] + bias_rows[0]).astype(BF) * BF(0.125)
    key_part = combined[:, width:2 * width].astype(BF)
    value_part = (combined[:, 2 * width:] + bias_rows[1]).astype(BF)
    partner_k = from_partner(key_part, "stream", 0)
    partner_v = from_partner(value_part, "stream", 0)
    e, et, qseg, kseg = prepare(segment_ids, box_cells[0], distance_table[0], is_vision)
    onehot = code_onehot()
    bt = jnp.dot(distance_table[0].T.astype(BF), onehot, preferred_element_type=jnp.float32).astype(BF).reshape(heads, 256, 256)
    attended, qmisc = fwd(queries, key_part, partner_k, value_part, partner_v, e, bt, qseg, kseg, length)
    vec = jnp.concatenate([bias_rows[2:3], norm_gains[1:2], norm_shifts[1:2], down_bias, jnp.zeros((4, width), F32)])
    q_send, m_send = lax.optimization_barrier((queries, qmisc))
    partner_q = from_partner(q_send, "stream", 0)
    partner_m = from_partner(m_send, "stream", 0)
    group = lax.axis_size("batch")
    (output, grad_middle, grad_attended, dmisc, grad_out, grad_up, grad_down, grad_up_bias, small_mid, segs) = mid(
        features[0].reshape(tokens, width), cotangent[0].reshape(tokens, width), attended, out_weight, vec,
        up_weight, down_weight, up_bias, group, 5)
    output = output.reshape(1, rows, length, width)
    small_up = grad_up_bias.reshape(-1, 128)
    early = jnp.concatenate([small_mid.reshape(-1, 128), small_up])
    vec_one = jnp.concatenate([norm_gains[0:1], norm_shifts[0:1], jnp.zeros((6, width), F32)])
    input_grad, small_a, small_b, sum_up, sum_down, sum_out, sum_qkv = back(
        queries, key_part, partner_k, value_part, partner_v, grad_attended, dmisc, qmisc, e, et, bt, kseg,
        partner_q, partner_m, features[0].reshape(tokens, width), qkv_weight, grad_middle, vec_one, early,
        segs, [grad_up, grad_down, grad_out], up_weight.shape[1], length, group, 4)
    input_grad = input_grad.reshape(1, rows, length, width)
    tab_rows = 16 * heads
    by_gap = small_a[:tab_rows, :16].reshape(heads, 2, GRID, 16)
    turn = jnp.arange(16)
    reach = jnp.minimum(jnp.stack([turn, 16 - turn]), GRID - 1)
    near = (reach[:, :, None] == jnp.arange(GRID)).astype(F32)
    dist = jnp.einsum("hpyd,pdx->xyh", by_gap, near, precision=lax.Precision.HIGHEST).reshape(1, GRID * GRID, heads)
    mid_sums = small_a[tab_rows:tab_rows + 8 * width // 128].reshape(8, width)
    upb = small_a[tab_rows + 8 * width // 128:].reshape(1, -1)
    last = small_b.reshape(4, width)
    gain = jnp.stack([last[0], mid_sums[0]])[None]
    shift = jnp.stack([last[1], mid_sums[1]])[None]
    bias = jnp.stack([last[2], last[3], mid_sums[2]])[None]
    downb = mid_sums[3][None]
    f32 = lambda a: a.astype(jnp.float32)[None]
    return (output, input_grad, gain, shift, f32(sum_qkv), bias, dist, f32(sum_out), f32(sum_up), upb, f32(sum_down), downb)


def solution(mesh):
    in_specs = (
        P("stream", "batch", None, None),
        P("stream", "batch", None, None),
        P("batch", None),
        P("stream", "batch", None, None),
        P("stream", None, None),
        P("stream", None, None),
        P("stream", None, None),
        P("stream", None, None),
        P("stream", None, None),
        P("stream", None, None),
        P("stream", None, None),
        P("stream", None),
        P("stream", None, None),
        P("stream", None),
    )
    out_specs = (
        P("stream", "batch", None, None),
        P("stream", "batch", None, None),
        P("stream", None, None),
        P("stream", None, None),
        P("stream", None, None),
        P("stream", None, None),
        P("stream", None, None),
        P("stream", None, None),
        P("stream", None, None),
        P("stream", None),
        P("stream", None, None),
        P("stream", None),
    )
    return jax.shard_map(
        on_device, mesh=mesh, in_specs=in_specs, out_specs=out_specs, check_vma=False
    )
```

profile of v0, /device:TPU:0, one launch (start us, length us, event | category | flops | bytes accessed | tf_op | source)
XLA Modules:
  0.0 434.1 jit_solution(13370715867845683107)
XLA Ops:
  0.6 0.0 copy-start.4
  0.7 0.0 copy-start.10
  0.7 0.0 copy-start.12
  0.7 0.0 copy-start.13
  0.7 0.0 copy-start.6
  0.7 1.8 convert_reduce_fusion
  2.5 2.1 fusion.3
  4.7 0.0 copy-done.10
  4.8 0.0 copy-done.12
  4.8 0.0 copy-done.13
  4.8 0.6 fusion.6
  5.5 3.8 fusion.41
  9.3 1.6 fusion.43
  10.9 2.9 collective-permute-start
  13.8 0.3 fusion.7.vn_ref
  14.1 0.0 copy-start.5
  14.1 0.1 collective-permute-start.1
  14.2 0.2 fusion.24
  14.4 2.6 convolution_convert_fusion
  17.1 0.0 copy-start.16
  17.1 0.0 copy-start.11
  17.1 0.5 copy.32
  17.5 1.3 slice.155.b_ref
  18.8 0.2 compare_convert_fusion.qseg_ref
  19.1 0.2 select_convert_fusion.kseg_ref
  19.3 0.2 fusion.10.e_ref
  19.5 0.0 copy-start.1
  19.5 29.7 %collective-permute-done.kf_ref = bf16[1024,768]{1,0:T(8,128)(2,1)} collective-permute-done((bf16[1024,768]{1,0:T(8,128)(2,1)S(1)}, bf16[1024,768]{1,0:T(8,128)(2,1)}, u32[]{:S(2)}, u32[]{:S(2)}) %collective-permute-start) | collective-permute-done | bytes 1572896 | tf_op jit(solution)/shard_map/ppermute | solution.py:532
  49.2 32.9 %collective-permute-done.1.vf_ref = bf16[1024,768]{1,0:T(8,128)(2,1)} collective-permute-done((bf16[1024,768]{1,0:T(8,128)(2,1)S(1)}, bf16[1024,768]{1,0:T(8,128)(2,1)}, u32[]{:S(2)}, u32[]{:S(2)}) %collective-permute-start.1) | collective-permute-done | bytes 1572896 | tf_op jit(solution)/shard_map/ppermute | solution.py:532
  82.0 0.0 copy-done
  82.0 33.4 %att_fwd.1 = (bf16[1024,768]{1,0:T(8,128)(2,1)S(1)}, bf16[1024,128]{1,0:T(8,128)(2,1)}) custom-call(bf16[1024,768]{1,0:T(8,128)(2,1)} %get-tuple-element.38.q_ref, bf16[1024,768]{1,0:T(8,128)(2,1)S(1)} %get-tuple-element.68.kn_ref, bf16[1024,768]{1,0:T(8,128)(2,1)} %collective-permute-done.kf_ref, bf16[1024,768]{1,0:T(8,128)(2,1)} %copy-done.5, ...), custom_call_target="tpu_custom_call" | custom-call | tf_op jit(solution)/shard_map/att_fwd/pallas_call | solution.py:60
  115.4 0.0 copy-start.3
  115.4 1.1 copy-done.3
  116.6 1.7 collective-permute-start.2
  118.3 0.1 pad.13.clone
  118.4 0.7 maximum_maximum_fusion.vec_ref
  119.1 0.9 fusion.11.et_ref
  120.0 0.3 collective-permute-start.3
  120.3 0.6 concatenate.13.vec_ref
  120.9 0.6 add_minimum_fusion
  121.5 111.5 %feed_forward.1 = (bf16[1024,768]{1,0:T(8,128)(2,1)}, f32[1024,768]{1,0:T(8,128)}, bf16[1024,768]{1,0:T(8,128)(2,1)}, bf16[1024,128]{1,0:T(8,128)(2,1)}, bf16[76...) custom-call(bf16[1024,768]{1,0:T(8,128)(2,1)} %bitcast.110, ...), custom_call_target="tpu_custom_call" | custom-call | tf_op jit(solution)/shard_map/feed_forward/pallas_call | solution.py:515
  233.1 0.7 reshape.242
  233.8 1.3 pad_maximum_fusion.early_ref
  235.1 0.0 collective-permute-done.3.qmf_ref
  235.1 0.0 collective-permute-done.2.qf_ref
  235.1 169.5 %att_bwd.1 = (bf16[1024,768]{1,0:T(8,128)(2,1)}, f32[264,128]{1,0:T(8,128)}, f32[24,128]{1,0:T(8,128)}, bf16[768,3072]{1,0:T(8,128)(2,1)}, bf16[3072,768]{1,0:T(...) custom-call(bf16[1024,768]{1,0:T(8,128)(2,1)} %get-tuple-element.38.q_ref, bf16[1024,768]{1,0:T(8,128)(2,1)} %copy-done, ...), custom_call_target="tpu_custom_call" | custom-call | tf_op jit(solution)/shard_map/att_bwd/pallas_call | solution.py:388
  404.6 0.8 slice_bitcast_fusion
  405.4 0.9 slice.146
  406.3 1.3 slice.147
  407.6 0.8 slice_bitcast_fusion.3
  408.4 0.0 copy-start.15
  408.4 5.6 %bitcast_convert_fusion.2 = f32[1,768,2304]{2,1,0:T(8,128)} fusion(bf16[768,2304]{1,0:T(8,128)(2,1)} %get-tuple-element.50), kind=kLoop, calls=%fused_computation.9 | loop fusion | flops 1769472 | bytes 10616832 | tf_op jit(solution)/shard_map/broadcast_in_dim | solution.py:626
  414.0 0.6 broadcast_in_dim.65
  414.7 0.4 convolution_bitcast_fusion
  415.0 0.1 copy.28
  415.1 0.7 reshape.254
  415.8 1.6 bitcast_convert_fusion.3
  417.4 7.9 %bitcast_convert_fusion.1 = f32[1,768,3072]{2,1,0:T(8,128)} fusion(bf16[768,3072]{1,0:T(8,128)(2,1)} %get-tuple-element.52), kind=kLoop, calls=%fused_computation.4 | loop fusion | flops 2359296 | bytes 14155776 | tf_op jit(solution)/shard_map/broadcast_in_dim | solution.py:626
  425.3 4.5 %bitcast_convert_fusion = f32[1,3072,768]{2,1,0:T(8,128)} fusion(bf16[3072,768]{1,0:T(8,128)(2,1)S(1)} %bitcast.114), kind=kLoop, calls=%fused_computation.3 | loop fusion | flops 2359296 | bytes 14155776 | tf_op jit(solution)/shard_map/broadcast_in_dim | solution.py:626
  429.8 0.6 copy.56
  430.4 0.6 maximum_bitcast_fusion
  431.0 0.6 maximum_bitcast_fusion.1
  431.6 1.1 copy.66
  432.8 1.1 copy.67
  (46 shorter events, 0.2 us)
Async XLA Ops:
  0.6 4.2 copy-start.4
  0.7 4.1 copy-start.10
  0.7 4.1 copy-start.12
  0.7 4.1 copy-start.13
  0.7 4.8 %copy-start.6 = (bf16[1,768,2304]{2,1,0:T(8,128)(2,1)S(1)}, bf16[1,768,2304]{2,1,0:T(8,128)(2,1)}, u32[]{:S(2)}) copy-start(bf16[1,768,2304]{2,1,0:T(8,128)(2,1)} %param.20) | copy-start | bytes 10616836
  10.9 71.1 %copy-start = (bf16[1024,768]{1,0:T(8,128)(2,1)}, bf16[1024,768]{1,0:T(8,128)(2,1)S(1)}, u32[]{:S(2)}) copy-start(bf16[1024,768]{1,0:T(8,128)(2,1)S(1)} %get-tuple-element.68.kn_ref) | copy-start | bytes 4718596
  10.9 3.5 copy-start.14
  10.9 38.3 %collective-permute-start = (bf16[1024,768]{1,0:T(8,128)(2,1)S(1)}, bf16[1024,768]{1,0:T(8,128)(2,1)}, u32[]{:S(2)}, u32[]{:S(2)}) collective-permute-start(bf16[1024,768]{1,0:T(8,128)(2,1)S(1)} %get-tuple-element.68.kn_ref), channel_id=1, source_target_pairs={{0,16},{16,0},{1,17},{17,1},{2,18},{18,2},{3,19},{19,3},{4,20},{20... | collective-permute-start | bytes 4718600 | tf_op jit(solution)/shard_map/ppermute | solution.py:532
  14.1 2.9 copy-start.5
  14.1 67.9 %collective-permute-start.1 = (bf16[1024,768]{1,0:T(8,128)(2,1)S(1)}, bf16[1024,768]{1,0:T(8,128)(2,1)}, u32[]{:S(2)}, u32[]{:S(2)}) collective-permute-start(bf16[1024,768]{1,0:T(8,128)(2,1)S(1)} %fusion.7.vn_ref), channel_id=1, source_target_pairs={{0,16},{16,0},{1,17},{17,1},{2,18},{18,2},{3,19},{19,3},{4,20},{20... | collective-permute-start | bytes 4718600 | tf_op jit(solution)/shard_map/ppermute | solution.py:532
  17.1 1.7 copy-start.16
  17.1 1.8 copy-start.11
  19.3 96.1 %copy-start.2 = (bf16[1024,128]{1,0:T(8,128)(2,1)}, bf16[1024,128]{1,0:T(8,128)(2,1)S(1)}, u32[]{:S(2)}) copy-start(bf16[1024,128]{1,0:T(8,128)(2,1)S(1)} %select_convert_fusion.kseg_ref) | copy-start | bytes 786436
  19.5 95.9 %copy-start.1 = (bf16[1024,256]{1,0:T(8,128)(2,1)}, bf16[1024,256]{1,0:T(8,128)(2,1)S(1)}, u32[]{:S(2)}) copy-start(bf16[1024,256]{1,0:T(8,128)(2,1)S(1)} %fusion.10.e_ref) | copy-start | bytes 1572868
  82.0 38.2 %copy-start.17 = (f32[1,768]{1,0:T(1,128)S(1)}, f32[1,768]{1,0:T(1,128)}, u32[]{:S(2)}) copy-start(f32[1,768]{1,0:T(1,128)} %param.27) | copy-start | bytes 9220
  115.4 1.1 copy-start.3
  116.6 118.6 %collective-permute-start.2 = (bf16[1024,768]{1,0:T(8,128)(2,1)}, bf16[1024,768]{1,0:T(8,128)(2,1)}, u32[]{:S(2)}, u32[]{:S(2)}) collective-permute-start(bf16[1024,768]{1,0:T(8,128)(2,1)} %get-tuple-element.38.q_ref), channel_id=1, source_target_pairs={{0,16},{16,0},{1,17},{17,1},{2,18},{18,2},{3,19},{19,3},{4,20},{20... | collective-permute-start | bytes 4718600 | tf_op jit(solution)/shard_map/ppermute | solution.py:532
  120.0 115.1 %collective-permute-start.3 = (bf16[1024,128]{1,0:T(8,128)(2,1)}, bf16[1024,128]{1,0:T(8,128)(2,1)}, u32[]{:S(2)}, u32[]{:S(2)}) collective-permute-start(bf16[1024,128]{1,0:T(8,128)(2,1)} %get-tuple-element.39.qm_ref), channel_id=1, source_target_pairs={{0,16},{16,0},{1,17},{17,1},{2,18},{18,2},{3,19},{19,3},{4,20},{20... | collective-permute-start | bytes 786440 | tf_op jit(solution)/shard_map/ppermute | solution.py:532
  408.4 6.2 %copy-start.15 = (s32[2,16]{1,0:T(2,128)S(1)}, s32[2,16]{1,0:T(2,128)}, u32[]{:S(2)}) copy-start(s32[2,16]{1,0:T(2,128)} %add_minimum_fusion) | copy-start | bytes 388
  408.4 7.4 %copy-start.9 = (bf16[768,768]{1,0:T(8,128)(2,1)S(1)}, bf16[768,768]{1,0:T(8,128)(2,1)}, u32[]{:S(2)}) copy-start(bf16[768,768]{1,0:T(8,128)(2,1)} %get-tuple-element.51) | copy-start | bytes 3538948
  415.8 9.5 %slice-start = ((s8[4718592]{0:T(1024)(128)(4,1)}), s8[4194304]{0:T(1024)(128)(4,1)S(1)}, s32[]{:S(2)}) async-start(s8[4718592]{0:T(1024)(128)(4,1)} %bitcast.113), calls=%async_computation | async-start | bytes 8388608
  417.4 7.9 %slice-start.1 = ((s8[4718592]{0:T(1024)(128)(4,1)}), s8[524288]{0:T(1024)(128)(4,1)S(1)}, s32[]{:S(2)}) async-start(s8[4718592]{0:T(1024)(128)(4,1)} %bitcast.113), calls=%async_computation.1 | async-start | bytes 1048576
  425.3 6.3 %copy-start.7 = (bf16[1024,768]{1,0:T(8,128)(2,1)S(1)}, bf16[1024,768]{1,0:T(8,128)(2,1)}, u32[]{:S(2)}) copy-start(bf16[1024,768]{1,0:T(8,128)(2,1)} %get-tuple-element.34) | copy-start | bytes 4718596
  429.8 2.9 copy-start.8
where the time goes:
time: 443 us; the launch traced here: 434 us
  Pallas kernels  314 us (71%)
  waiting for transfers between devices  62.5 us (14%)
  other arithmetic  31.6 us (7%)
  local copies, waits for them, and re-layouts  12.5 us (3%)
  matrix products  6.8 us (2%)
  starting transfers between devices  5.04 us (1%)
    pallas_call x1, Pallas kernels, back(): pl.pallas_call(functools.partial(back_kernel, n, NP, R, chunks, loads, cu...  169 us
    pallas_call x1, Pallas kernels, mid(): pl.pallas_call(functools.partial(mid_kernel, n, chunks, TILES), grid=(TIL...  112 us
    ppermute x4, waiting for transfers between devices, from_partner(): return lax.ppermute(block, axis, route)  62.5 us
    pallas_call x1, Pallas kernels, fwd(): pl.pallas_call(functools.partial(fwd_kernel, CQ), grid=(R, NP), in_specs=...  33.4 us
    broadcast_in_dim x4, other arithmetic, on_device(): f32 = lambda a: a.astype(jnp.float32)[None]  19.5 us
  transfers between devices with their start and end apart: 4, of which 2 were waited for; matrix products, arithmetic and copies ran while one was open for 2% of the time, Pallas kernels for 26%

commit v1 on v0

--- a/solution.py
+++ b/solution.py
@@ -93,8 +93,8 @@
     return pl.ds(off if isinstance(off,int) else pl.multiple_of(off,16),size)
 
 class Engine:
-    def __init__(self, n, me, lag, chunks, x, recv, segs, sums, ss, rs, os):
-        self.me,self.lag,self.chunks=me,lag,chunks
+    def __init__(self, n, me, chunks, x, recv, segs, sums, ss, rs, os):
+        self.me,self.chunks=me,chunks
         self.x,self.recv,self.segs,self.sums=x,recv,segs,sums
         self.ss,self.rs,self.os=ss,rs,os
         self.bits=n.bit_length()-1
@@ -169,18 +169,27 @@
             if stage==self.bits-1 and self.chunks[c]["last"]==self.bits:
                 self.segs[self.chunks[c]["seg"]]=x[h,rows_at(off,m)]
 
+    def times(self,c):
+        ch=self.chunks[c]
+        order=bit_order(self.n,ch["kind"]); order=order+order[::-1]
+        at=[ch["entry"]]
+        for s in range(ch["first"],ch["last"]): at.append(at[-1]+(1 if order[s]==0 else LAG))
+        return at
+
     def slot(self,t,load):
-        for c in sorted(range(len(self.chunks)),key=lambda c:self.chunks[c]["entry"]):
+        todo=[]
+        for c in range(len(self.chunks)):
+            at=self.times(c)
+            if t in at:
+                todo.append((self.chunks[c]["entry"],c,self.chunks[c]["first"]+at.index(t)))
+        for _,c,s in sorted(todo):
             ch=self.chunks[c]
-            if t<ch["entry"] or (t-ch["entry"])%self.lag: continue
-            s=ch["first"]+(t-ch["entry"])//self.lag
-            if s>ch["last"]: continue
             if s==ch["first"]: load(c)
             else: self.finish(c,s-1)
             if s<ch["last"]: self.start(c,s)
 
     def end(self):
-        return 1+max(ch["entry"]+self.lag*(ch["last"]-ch["first"]) for ch in self.chunks)
+        return 1+max(self.times(c)[-1] for c in range(len(self.chunks)))
 
 def small_copy(me,x,recv,ss,rs,s):
     return pltpu.make_async_remote_copy(x.at[s],recv.at[s],ss.at[s],rs.at[s],device_id={"batch":place(me,s)[1]},device_id_type=MESH)
@@ -188,9 +197,9 @@
 def back_kernel(n, NP, R, chunks, loads, cuts,
                q_ref,kn_ref,kf_ref,vn_ref,vf_ref,do_ref,dm_ref,qm_ref,e_ref,et_ref,b_ref,kseg_ref,qf_ref,qmf_ref,
                feat_ref,wqkv_ref,gm_ref,vec_ref,early_ref,
-               do_any,dm_any,segs,gu_any,gd_any,go_any,
-               ig_ref,smalla_ref,smallb_ref,su_any,sd_any,so_any,sq_any,
-               dof,dmf,gmix,nt_s,g_s,tab,x,recv,ax,arecv,bx,brecv,in_sem,out_sem,ss,rs,xs_sem,xr_sem,a_ss,a_rs,b_ss,b_rs):
+               do_any,dm_any,gu_any,gd_any,go_any,
+               ig_ref,small_ref,su_any,sd_any,so_any,sq_any,
+               dof,dmf,gmix,nt_s,g_s,tab,x,recv,ax,arecv,in_sem,out_sem,ss,rs,xs_sem,xr_sem,a_ss,a_rs):
     step=pl.program_id(0)
     per=NP*R
     second=(step>=per)&(step<2*per)
@@ -201,12 +210,12 @@
     zero=jnp.zeros((),BF)
     RC=256
     grads=(gu_any,gd_any,go_any)
-    eng=Engine(n,me,LAG,chunks,x,recv,segs,(su_any,sd_any,so_any,sq_any),ss,rs,out_sem)
+    eng=Engine(n,me,chunks,x,recv,None,(su_any,sd_any,so_any,sq_any),ss,rs,out_sem)
     B=eng.bits
     q_set,mid_set,end_set=[[c for c in range(len(chunks)) if chunks[c].get("set")==i] for i in range(3)]
     def load(c):
-        a,k=loads[c]
-        return pltpu.make_async_copy(grads[a].at[:,pl.ds(k*WIDE,WIDE)],x.at[chunks[c]["slot"]],in_sem.at[c])
+        a,i,k=loads[c]
+        return pltpu.make_async_copy(grads[a].at[pl.ds(i*SIDE,SIDE),pl.ds(k*WIDE,WIDE)],x.at[chunks[c]["slot"]],in_sem.at[c])
     def ready(c):
         if c in loads: load(c).wait()
     def across():
@@ -232,9 +241,8 @@
     def tick(half):
         for k in range(2*per):
             i=k*2+half
-            small_now=half==0 and k>=per and k-per<=B
             group=q_set if i==2*per else mid_set if i==3*per else []
-            if edges[i]==edges[i+1] and not small_now and not group: continue
+            if edges[i]==edges[i+1] and not group: continue
             @pl.when(step==k)
             def _():
                 if i==2*per:
@@ -244,17 +252,6 @@
                         nt_s[:,sl]=(nrm*vec_ref[0:1,:]+vec_ref[1:2,:]).astype(BF).T
                 for c in group: form(c)
                 for t in range(edges[i],edges[i+1]): eng.slot(t,ready)
-                if small_now:
-                    s=k-per
-                    if s==0:
-                        put=(lax.broadcasted_iota(jnp.int32,(256,128),1)==lax.broadcasted_iota(jnp.int32,(256,128),0)//16).astype(BF)
-                        ax[0,:2*NP*16]=sum(mm(v,put) for v in three(tab[...]))
-                        ax[0,2*NP*16:]=early_ref[...]
-                    else:
-                        small_copy(me,ax,arecv,a_ss,a_rs,s-1).wait()
-                        ax[s]=ax[s-1]+arecv[s-1]
-                    if s<B: small_copy(me,ax,arecv,a_ss,a_rs,s).start()
-                    else: smalla_ref[...]=ax[B]
     def half_of(hh):
         return (lane<64) if hh==0 else (lane>=64)
     def ones_of(h):
@@ -335,23 +332,26 @@
             qg=g*vec_ref[0:1,:]
             ig_ref[sl,:]=(gm_ref[sl,:]+(qg-jnp.mean(qg,axis=1,keepdims=True)-nrm*jnp.mean(qg*nrm,axis=1,keepdims=True))*inv).astype(BF)
             eng.slot(now,ready); now+=1
-        w=D//128
+        w=D//128; base=2*NP*16+early_ref.shape[0]
         for i,v in enumerate((gain,shift,qb,vb)):
-            for k in range(w): bx[0,i*w+k:i*w+k+1,:]=v[:,k*128:(k+1)*128]
-        small_copy(me,bx,brecv,b_ss,b_rs,0).start()
+            for k in range(w): ax[0,base+i*w+k:base+i*w+k+1,:]=v[:,k*128:(k+1)*128]
+        put=(lax.broadcasted_iota(jnp.int32,(256,128),1)==lax.broadcasted_iota(jnp.int32,(256,128),0)//16).astype(BF)
+        ax[0,:2*NP*16]=sum(mm(v,put) for v in three(tab[...]))
+        ax[0,2*NP*16:base]=early_ref[...]
+        small_copy(me,ax,arecv,a_ss,a_rs,0).start()
         done=1
         for t in range(now,max(eng.end(),now+LAG*B)):
             eng.slot(t,ready)
             if (t-now)%LAG==LAG-1 and done<=B:
-                small_copy(me,bx,brecv,b_ss,b_rs,done-1).wait()
-                bx[done]=bx[done-1]+brecv[done-1]
-                if done<B: small_copy(me,bx,brecv,b_ss,b_rs,done).start()
+                small_copy(me,ax,arecv,a_ss,a_rs,done-1).wait()
+                ax[done]=ax[done-1]+arecv[done-1]
+                if done<B: small_copy(me,ax,arecv,a_ss,a_rs,done).start()
                 done+=1
         assert done==B+1
-        smallb_ref[...]=bx[B]
+        small_ref[...]=ax[B]
         for d in across(): d.wait_send()
 
-def back(q,kn,kf,vn,vf,do,dm,qmisc,e,et,bt,kseg,qf,qmf,feat,wqkv,gm,vec,early,segs,grads,full_ff,L,n,collective_id):
+def back(q,kn,kf,vn,vf,do,dm,qmisc,e,et,bt,kseg,qf,qmf,feat,wqkv,gm,vec,early,grads,L,n,collective_id):
     T,D=q.shape; R=T//L; NP=D//128; per=R*NP
     def one(step): i=jnp.minimum(step,per-1); return i%R,i//R
     def cyc(step): i=jnp.minimum(step,2*per-1)%per; return i%R,i//R
@@ -361,19 +361,22 @@
     full=lambda a: pl.BlockSpec(a.shape,lambda s:(0,)*len(a.shape),pipeline_mode=pl.Buffered(1))
     any_=pl.BlockSpec(memory_space=pl.ANY)
     S=jax.ShapeDtypeStruct; sem=pltpu.SemaphoreType.DMA
-    bits=n.bit_length()-1; per_side=D//WIDE; tiles=full_ff//SIDE
-    first=max(20,LAG*(bits+1)+per_side)
-    cuts=(first,first+9,first+20)
+    bits=n.bit_length()-1; per_side=D//WIDE; full_ff=grads[0].shape[1]; tiles=full_ff//SIDE; early_tiles=0
+    count=per_side*(2*tiles+1)
+    cuts=(count,count+per_side,count+2*per_side)
     chunks=[]; loads={}
     def chunk(to,entry,**more):
         ch=dict(to=to,entry=entry,kind=len(chunks),first=0,last=2*bits); ch.update(more); chunks.append(ch)
-    for i,(a,r,k) in enumerate([(0,0,(tiles-1)*per_side+k) for k in range(per_side)]+[(1,tiles-1,k) for k in range(per_side)]+[(2,0,k) for k in range(per_side)]):
-        loads[len(chunks)]=(a,i%per_side)
-        chunk((a,r,k),3*i,slot=i,land=i)
-    place_of=[p for t in range(tiles-1) for p in [(0,0,t*per_side+k) for k in range(per_side)]+[(1,t,k) for k in range(per_side)]]
-    spare=[t for t in range(first) if t%3 or t>=3*len(loads)]
+    late=[]
+    for t in range(early_tiles,tiles):
+        late+=[(0,0,t*per_side+k) for k in range(per_side)]+[(1,t,k) for k in range(per_side)]
+    late+=[(2,0,k) for k in range(per_side)]
+    for i,(a,r,k) in enumerate(late):
+        loads[len(chunks)]=(a,r-early_tiles if a==1 else 0,k-early_tiles*per_side if a==0 else k)
+        chunk((a,r,k),i,slot=i,land=i)
+    place_of=[p for t in range(early_tiles) for p in [(0,0,t*per_side+k) for k in range(per_side)]+[(1,t,k) for k in range(per_side)]]
     for i,p in enumerate(place_of):
-        chunk(p,spare[i],first=bits,seg=i,kind=i)
+        chunk(p,2*i+1,first=bits,seg=i,kind=i)
     at=len(loads)
     half=per_side//2
     for g,group in enumerate(([k for k in range(per_side)],[per_side+k for k in range(half)]+[2*per_side+k for k in range(half)],
@@ -382,21 +385,21 @@
             chunk((3,0,k),cuts[g]+i,slot=at,land=at,set=g); at+=1
     C=len(chunks)
     rows=sum(plan_of(bits,SIDE)[1:])
-    asmall=(2*NP*16+early.shape[0],128); bsmall=(4*D//128,128)
-    outs=[S((T,D),BF),S(asmall,F32),S(bsmall,F32)]
+    asmall=(2*NP*16+early.shape[0]+4*D//128,128)
+    outs=[S((T,D),BF),S(asmall,F32)]
     sums=[S((D,full_ff),BF),S((full_ff,D),BF),S((D,D),BF),S(wqkv.shape,BF)]
     return pl.pallas_call(functools.partial(back_kernel,n,NP,R,chunks,loads,cuts),grid=(2*per+1,),
         in_specs=[blk(one),blk(cyc),blk(one),blk(cyc),blk(one),blk(one),row(128,one),row(128,one),row(256,one),
                   pl.BlockSpec((256,L),lambda s:(0,one(s)[0])),pl.BlockSpec((2,256,256),lambda s:(one(s)[1],0,0)),row(128,one),blk(two),row(128,two),
-                  full(feat),full(wqkv),full(gm),full(vec),full(early)]+[any_]*2+[full(segs)]+[any_]*3,
+                  full(feat),full(wqkv),full(gm),full(vec),full(early)]+[any_]*5,
         out_specs=[full(o) for o in outs]+[any_]*4,
         out_shape=outs+sums,
         scratch_shapes=[pltpu.VMEM((NP,T,128),BF),pltpu.VMEM((T,128),BF),pltpu.VMEM((T,3*D),BF),pltpu.VMEM((D,T),BF),pltpu.VMEM((2,256,256),F32),pltpu.VMEM((2*NP*16,256),F32),
             pltpu.VMEM((at,SIDE,WIDE),BF),pltpu.VMEM((at,rows,WIDE),BF),
-            pltpu.VMEM((bits+1,)+asmall,F32),pltpu.VMEM((bits,)+asmall,F32),pltpu.VMEM((bits+1,)+bsmall,F32),pltpu.VMEM((bits,)+bsmall,F32),
-            sem((C,)),sem((C,)),sem((C,2*bits)),sem((C,2*bits)),sem((NP+1,)),sem((NP+1,)),sem((bits,)),sem((bits,)),sem((bits,)),sem((bits,))],
+            pltpu.VMEM((bits+1,)+asmall,F32),pltpu.VMEM((bits,)+asmall,F32),
+            sem((C,)),sem((C,)),sem((C,2*bits)),sem((C,2*bits)),sem((NP+1,)),sem((NP+1,)),sem((bits,)),sem((bits,))],
         compiler_params=pltpu.CompilerParams(collective_id=collective_id,has_side_effects=True,vmem_limit_bytes=64<<20),
-        name="att_bwd")(q,kn,kf,vn,vf,do,dm,qmisc,e,et,bt,kseg,qf,qmf,feat,wqkv,gm,vec,early,do,dm,segs,*grads)
+        name="att_bwd")(q,kn,kf,vn,vf,do,dm,qmisc,e,et,bt,kseg,qf,qmf,feat,wqkv,gm,vec,early,do,dm,*grads)
 
 
 def gelu_both(u):
@@ -415,111 +418,77 @@
 
 def colsum(v): return jnp.sum(v,axis=0,keepdims=True)
 
-
-MID_LAG=2
-def mid_kernel(n, chunks, TILES, x_ref,cot_ref,att_ref,wo_ref,vec_ref,wu_ref,wd_ref,ub_ref,
-               out_ref,gm_ref,do_ref,dm_ref,gwo_ref,gul_ref,gdl_ref,gub_ref,small_ref,seg_ref,
-               mid_s,nt_s,ntt_s,acc_s,gn_s,act_s,gp_s,x,recv,ss,rs):
-    j=pl.program_id(0); T=x_ref.shape[0]; D=x_ref.shape[1]; RC=256
-    parts=[slice(i*RC,(i+1)*RC) for i in range(T//RC)]
-    me=lax.axis_index("batch")
-    eng=Engine(n,me,MID_LAG,chunks,x,recv,seg_ref,None,ss,rs,None)
-    per_tile=2*D//WIDE; pace=2*len(parts)
-    def tick(i):
-        for jj in range(1,TILES):
-            @pl.when(j==jj)
-            def _():
-                for t in range(2*i,2*i+2): eng.slot(pace*(jj-1)+t,lambda c:None)
+def mid_kernel(RC, x_ref,cot_ref,att_ref,wo_ref,vec_ref,wu_ref,wd_ref,ub_ref,
+               out_ref,gm_ref,do_ref,dm_ref,gwo_ref,gwu_ref,gwd_ref,gub_ref,small_ref,
+               mid_s,nt_s,ntt_s,acc_s,gn_s):
+    j=pl.program_id(0); T=x_ref.shape[0]; NTL=pl.num_programs(0)
+    chunks=[slice(i*RC,(i+1)*RC) for i in range(T//RC)]
     @pl.when(j==0)
     def _():
-        sem=pltpu.get_barrier_semaphore()
-        for b in range(eng.bits):
-            pl.semaphore_signal(sem,inc=1,device_id={"batch":place(me,b)[1]},device_id_type=MESH)
-        for sl in parts:
+        for sl in chunks:
             v=x_ref[sl,:].astype(F32)+mm(att_ref[sl,:],wo_ref[...])+vec_ref[0:1,:]
             mid_s[sl,:]=v
-            nrm,_=norm_parts(v)
-            nt=(nrm*vec_ref[1:2,:]+vec_ref[2:3,:]).astype(BF)
+            n,_=norm_parts(v)
+            nt=(n*vec_ref[1:2,:]+vec_ref[2:3,:]).astype(BF)
             nt_s[sl,:]=nt
             ntt_s[:,sl]=nt.T
             acc_s[sl,:]=v+vec_ref[3:4,:]
             gn_s[sl,:]=jnp.zeros_like(v)
-        pl.semaphore_wait(sem,eng.bits)
-    gub=0.0
-    for i,sl in enumerate(parts):
-        tick(i)
+    gub=0.0; gwd=0.0; gwu=0.0
+    for sl in chunks:
         pre=mm(nt_s[sl,:],wu_ref[...])+ub_ref[...]
         act,slope=gelu_both(pre)
         act=act.astype(BF)
         gp=(mm(cot_ref[sl,:],wd_ref[...],NT)*slope).astype(BF)
-        act_s[sl,:]=act; gp_s[sl,:]=gp
         acc_s[sl,:]+=mm(act,wd_ref[...])
         gn_s[sl,:]+=mm(gp,wu_ref[...],NT)
         gub=gub+colsum(gp.astype(F32))
+        gwd=gwd+mm(act,cot_ref[sl,:],TN)
+        gwu=gwu+mm(ntt_s[:,sl],gp)
     gub_ref[...]=gub
-    for k in range(D//WIDE):
-        cs=slice(k*WIDE,(k+1)*WIDE)
-        up=mm(ntt_s[...],gp_s[:,cs]).astype(BF)
-        down=mm(act_s[...],cot_ref[:,cs],TN).astype(BF)
-        @pl.when(j<TILES-1)
-        def _():
-            x[per_tile*j+k]=up
-            x[per_tile*j+D//WIDE+k]=down
-        @pl.when(j==TILES-1)
-        def _():
-            gul_ref[:,cs]=up; gdl_ref[:,cs]=down
-    @pl.when(j==TILES-1)
+    gwd_ref[...]=gwd.astype(BF); gwu_ref[...]=gwu.astype(BF)
+    @pl.when(j==NTL-1)
     def _():
         g2=0.0; s2=0.0; ob=0.0; db=0.0; gwo=0.0
-        row=lax.broadcasted_iota(jnp.int32,(D,128),0)//64
-        col=lax.broadcasted_iota(jnp.int32,(D,128),1)
+        row=lax.broadcasted_iota(jnp.int32,(x_ref.shape[1],128),0)//64
+        col=lax.broadcasted_iota(jnp.int32,(x_ref.shape[1],128),1)
         pick=(row==col//3).astype(BF)
         lane=lax.broadcasted_iota(jnp.int32,(1,128),1)
-        now=pace*(TILES-1)
-        for sl in parts:
+        for sl in chunks:
             out_ref[sl,:]=acc_s[sl,:].astype(BF)
-            nrm,inv=norm_parts(mid_s[sl,:])
+            n,inv=norm_parts(mid_s[sl,:])
             q=gn_s[sl,:]
-            g2=g2+colsum(q*nrm); s2=s2+colsum(q)
+            g2=g2+colsum(q*n); s2=s2+colsum(q)
             qg=q*vec_ref[1:2,:]
             cot=cot_ref[sl,:].astype(F32)
             db=db+colsum(cot)
-            gm=cot+(qg-jnp.mean(qg,axis=1,keepdims=True)-nrm*jnp.mean(qg*nrm,axis=1,keepdims=True))*inv
+            gm=cot+(qg-jnp.mean(qg,axis=1,keepdims=True)-n*jnp.mean(qg*n,axis=1,keepdims=True))*inv
             gm_ref[sl,:]=gm
             gb=gm.astype(BF)
-            gp_s[sl,:]=gb
             ob=ob+colsum(gb.astype(F32))
             do=mm(gb,wo_ref[...],NT).astype(BF)
             do_ref[sl,:]=do
+            gwo=gwo+mm(att_ref[sl,:],gb,TN)
             prod=do.astype(F32)*att_ref[sl,:].astype(F32)
             hi=prod.astype(BF); lo=(prod-hi.astype(F32)).astype(BF)
             delta=-(mm(hi,pick)+mm(lo,pick))
             hi,md,lo=three(delta)
-            dm_ref[sl,:]=jnp.where(lane>=6*(D//128),jnp.zeros((),BF),jnp.where(lane%3==0,hi,jnp.where(lane%3==1,md,lo)))
-            eng.slot(now,lambda c:None); now+=1
-        gwo_ref[...]=mm(att_ref[...],gp_s[...],TN).astype(BF)
+            dm_ref[sl,:]=jnp.where(lane>=36,jnp.zeros((),BF),jnp.where(lane%3==0,hi,jnp.where(lane%3==1,md,lo)))
+        gwo_ref[...]=gwo.astype(BF)
         small_ref[0:1,:]=g2; small_ref[1:2,:]=s2; small_ref[2:3,:]=ob; small_ref[3:4,:]=db
-        small_ref[4:8,:]=jnp.zeros((4,D),F32)
-        for t in range(now,eng.end()): eng.slot(t,lambda c:None)
-
-def mid(x,cot,att,wo,vec,wu,wd,ub,n,collective_id):
-    T,D=x.shape; FF=wu.shape[1]; FT=SIDE; TILES=FF//FT
-    bits=n.bit_length()-1; pace=2*(T//256); per_tile=2*D//WIDE
-    sizes=plan_of(bits,SIDE)
-    chunks=[dict(entry=pace*(c//per_tile)+c%per_tile,kind=c,first=0,last=bits,slot=c,land=c,seg=c) for c in range(per_tile*(TILES-1))]
-    C=len(chunks)
-    one=lambda a: pl.BlockSpec(a.shape,lambda j:(0,)*len(a.shape),pipeline_mode=pl.Buffered(1))
-    S=jax.ShapeDtypeStruct; sem=pltpu.SemaphoreType.DMA
-    outs=[S((T,D),BF),S((T,D),F32),S((T,D),BF),S((T,128),BF),S((D,D),BF),S((D,D),BF),S((D,D),BF)]
-    tail=[S((8,D),F32),S((C,sizes[-1],WIDE),BF)]
-    return pl.pallas_call(functools.partial(mid_kernel,n,chunks,TILES),grid=(TILES,),
-        in_specs=[one(x),one(cot),one(att),one(wo),one(vec),pl.BlockSpec((D,FT),lambda j:(0,j)),pl.BlockSpec((FT,D),lambda j:(j,0)),pl.BlockSpec((1,FT),lambda j:(0,j))],
-        out_specs=[one(o) for o in outs]+[pl.BlockSpec((1,FT),lambda j:(0,j))]+[one(o) for o in tail],
-        out_shape=outs+[S((1,FF),F32)]+tail,
-        scratch_shapes=[pltpu.VMEM((T,D),F32),pltpu.VMEM((T,D),BF),pltpu.VMEM((D,T),BF),pltpu.VMEM((T,D),F32),pltpu.VMEM((T,D),F32),
-            pltpu.VMEM((T,FT),BF),pltpu.VMEM((T,FT),BF),
-            pltpu.VMEM((C,SIDE,WIDE),BF),pltpu.VMEM((C,sum(sizes[1:]),WIDE),BF),sem((C,bits)),sem((C,bits))],
-        compiler_params=pltpu.CompilerParams(collective_id=collective_id,has_side_effects=True,vmem_limit_bytes=64<<20),name="feed_forward")(x,cot,att,wo,vec,wu,wd,ub)
+        small_ref[4:8,:]=jnp.zeros((4,x_ref.shape[1]),F32)
+
+def mid(x,cot,att,wo,vec,wu,wd,ub,FT=512,RC=256):
+    T,D=x.shape; FF=wu.shape[1]
+    full=lambda a: pl.BlockSpec(a.shape,lambda j:(0,0))
+    S=jax.ShapeDtypeStruct
+    fs=lambda *s: pl.BlockSpec(s,lambda j:(0,0))
+    return pl.pallas_call(functools.partial(mid_kernel,RC),grid=(FF//FT,),
+        in_specs=[full(x),full(cot),full(att),full(wo),full(vec),pl.BlockSpec((D,FT),lambda j:(0,j)),pl.BlockSpec((FT,D),lambda j:(j,0)),pl.BlockSpec((1,FT),lambda j:(0,j))],
+        out_specs=[fs(T,D),fs(T,D),fs(T,D),fs(T,128),fs(D,D),pl.BlockSpec((D,FT),lambda j:(0,j)),pl.BlockSpec((FT,D),lambda j:(j,0)),pl.BlockSpec((1,FT),lambda j:(0,j)),fs(8,D)],
+        out_shape=[S((T,D),BF),S((T,D),F32),S((T,D),BF),S((T,128),BF),S((D,D),BF),S((D,FF),BF),S((FF,D),BF),S((1,FF),F32),S((8,D),F32)],
+        scratch_shapes=[pltpu.VMEM((T,D),F32),pltpu.VMEM((T,D),BF),pltpu.VMEM((D,T),BF),pltpu.VMEM((T,D),F32),pltpu.VMEM((T,D),F32)],
+        compiler_params=pltpu.CompilerParams(vmem_limit_bytes=60<<20),name="feed_forward")(x,cot,att,wo,vec,wu,wd,ub)
 
 
 def from_partner(block, axis, stride):
@@ -598,17 +567,17 @@
     partner_q = from_partner(q_send, "stream", 0)
     partner_m = from_partner(m_send, "stream", 0)
     group = lax.axis_size("batch")
-    (output, grad_middle, grad_attended, dmisc, grad_out, grad_up, grad_down, grad_up_bias, small_mid, segs) = mid(
+    (output, grad_middle, grad_attended, dmisc, grad_out, grad_up, grad_down, grad_up_bias, small_mid) = mid(
         features[0].reshape(tokens, width), cotangent[0].reshape(tokens, width), attended, out_weight, vec,
-        up_weight, down_weight, up_bias, group, 5)
+        up_weight, down_weight, up_bias)
     output = output.reshape(1, rows, length, width)
     small_up = grad_up_bias.reshape(-1, 128)
     early = jnp.concatenate([small_mid.reshape(-1, 128), small_up])
     vec_one = jnp.concatenate([norm_gains[0:1], norm_shifts[0:1], jnp.zeros((6, width), F32)])
-    input_grad, small_a, small_b, sum_up, sum_down, sum_out, sum_qkv = back(
+    input_grad, small_a, sum_up, sum_down, sum_out, sum_qkv = back(
         queries, key_part, partner_k, value_part, partner_v, grad_attended, dmisc, qmisc, e, et, bt, kseg,
         partner_q, partner_m, features[0].reshape(tokens, width), qkv_weight, grad_middle, vec_one, early,
-        segs, [grad_up, grad_down, grad_out], up_weight.shape[1], length, group, 4)
+        [grad_up, grad_down, grad_out], length, group, 4)
     input_grad = input_grad.reshape(1, rows, length, width)
     tab_rows = 16 * heads
     by_gap = small_a[:tab_rows, :16].reshape(heads, 2, GRID, 16)
@@ -617,8 +586,9 @@
     near = (reach[:, :, None] == jnp.arange(GRID)).astype(F32)
     dist = jnp.einsum("hpyd,pdx->xyh", by_gap, near, precision=lax.Precision.HIGHEST).reshape(1, GRID * GRID, heads)
     mid_sums = small_a[tab_rows:tab_rows + 8 * width // 128].reshape(8, width)
-    upb = small_a[tab_rows + 8 * width // 128:].reshape(1, -1)
-    last = small_b.reshape(4, width)
+    tail = small_a.shape[0] - 4 * width // 128
+    upb = small_a[tab_rows + 8 * width // 128:tail].reshape(1, -1)
+    last = small_a[tail:].reshape(4, width)
     gain = jnp.stack([last[0], mid_sums[0]])[None]
     shift = jnp.stack([last[1], mid_sums[1]])[None]
     bias = jnp.stack([last[2], last[3], mid_sums[2]])[None]

time: 443 us -> 402 us (0.907); the launches traced: 434 us -> 399 us
  Pallas kernels: 314 us -> 281 us
    pallas_call x1, Pallas kernels: 112 us -> 51.2 us  [mid(): pl.pallas_call(functools.partial(mid_kernel, RC), grid=(FF // FT,), in_sp...]
    pallas_call x1, Pallas kernels: 169 us -> 197 us  [back(): pl.pallas_call(functools.partial(back_kernel, n, NP, R, chunks, loads, cu...]
  transfers between devices with their start and end apart: 4 -> 4, of which waited for: 2 -> 2; matrix products, arithmetic and copies ran while one was open for 2% -> 3% of each run, Pallas kernels for 26% -> 13%
where the time goes in v1:
time: 402 us; the launch traced here: 399 us
  Pallas kernels  281 us (70%)
  waiting for transfers between devices  61.2 us (15%)
  other arithmetic  31.5 us (8%)
  local copies, waits for them, and re-layouts  11.9 us (3%)
  matrix products  6.8 us (2%)
  starting transfers between devices  5.37 us (1%)
    pallas_call x1, Pallas kernels, back(): pl.pallas_call(functools.partial(back_kernel, n, NP, R, chunks, loads, cu...  197 us
    ppermute x4, waiting for transfers between devices, from_partner(): return lax.ppermute(block, axis, route)  61.2 us
    pallas_call x1, Pallas kernels, mid(): pl.pallas_call(functools.partial(mid_kernel, RC), grid=(FF // FT,), in_sp...  51.2 us
    pallas_call x1, Pallas kernels, fwd(): pl.pallas_call(functools.partial(fwd_kernel, CQ), grid=(R, NP), in_specs=...  32.6 us
    broadcast_in_dim x4, other arithmetic, on_device(): f32 = lambda a: a.astype(jnp.float32)[None]  19.5 us
  transfers between devices with their start and end apart: 4, of which 2 were waited for; matrix products, arithmetic and copies ran while one was open for 3% of the time, Pallas kernels for 13%

profile of v1, /device:TPU:0, one launch (start us, length us, event | category | flops | bytes accessed | tf_op | source)
XLA Modules:
  0.0 399.3 jit_solution(1903837142692844537)
XLA Ops:
  0.6 0.0 copy-start.6
  0.7 0.0 copy-start.11
  0.7 0.0 copy-start.13
  0.7 0.0 copy-start.14
  0.7 0.0 copy-start.7
  0.7 1.8 convert_reduce_fusion
  2.5 2.1 fusion.3
  4.7 0.0 copy-done.11
  4.8 0.0 copy-done.13
  4.8 0.0 copy-done.14
  4.8 0.6 fusion.6
  5.5 3.8 fusion.41
  9.3 0.4 fusion.43
  9.8 0.0 copy-start.15
  9.8 3.0 collective-permute-start
  12.8 1.4 fusion.7.vn_ref
  14.2 0.3 collective-permute-start.1
  14.5 0.2 fusion.24
  14.8 2.6 convolution_convert_fusion
  17.4 0.0 copy-start.12
  17.4 0.5 copy.32
  17.9 1.3 slice.160.b_ref
  19.1 0.0 copy-done.17
  19.1 0.2 compare_convert_fusion.qseg_ref
  19.4 0.2 select_convert_fusion.kseg_ref
  19.6 0.0 copy-start.3
  19.6 0.2 fusion.10.e_ref
  19.8 28.3 %collective-permute-done.kf_ref = bf16[1024,768]{1,0:T(8,128)(2,1)} collective-permute-done((bf16[1024,768]{1,0:T(8,128)(2,1)S(1)}, bf16[1024,768]{1,0:T(8,128)(2,1)}, u32[]{:S(2)}, u32[]{:S(2)}) %collective-permute-start) | collective-permute-done | bytes 1572896 | tf_op jit(solution)/shard_map/ppermute | solution.py:501
  48.1 32.9 %collective-permute-done.1.vf_ref = bf16[1024,768]{1,0:T(8,128)(2,1)} collective-permute-done((bf16[1024,768]{1,0:T(8,128)(2,1)}, bf16[1024,768]{1,0:T(8,128)(2,1)}, u32[]{:S(2)}, u32[]{:S(2)}) %collective-permute-start.1) | collective-permute-done | bytes 1572896 | tf_op jit(solution)/shard_map/ppermute | solution.py:501
  81.0 32.6 %att_fwd.1 = (bf16[1024,768]{1,0:T(8,128)(2,1)S(1)}, bf16[1024,128]{1,0:T(8,128)(2,1)S(1)}) custom-call(bf16[1024,768]{1,0:T(8,128)(2,1)S(1)} %get-tuple-element.36.q_ref, bf16[1024,768]{1,0:T(8,128)(2,1)S(1)} %get-tuple-element.64.kn_ref, bf16[1024,768]{1,0:T(8,128)(2,1)} %collective-permute-done.kf_ref, bf16[1024,768]{1,0:T(8,128)(2,1)} %fusion.7.vn_ref, ...), custom_call_target="tpu_custom_call" | custom-call | tf_op jit(solution)/shard_map/att_fwd/pallas_call | solution.py:60
  113.6 0.0 copy-done.3
  113.7 0.0 copy-done.2
  113.7 0.0 copy-start.4
  113.7 1.2 copy-done.4
  114.8 1.7 collective-permute-start.2
  116.6 0.1 pad.13.clone
  116.7 0.7 maximum_maximum_fusion.vec_ref
  117.3 0.9 fusion.11.et_ref
  118.2 0.3 collective-permute-start.3
  118.5 0.6 concatenate.13.vec_ref
  119.2 0.6 add_minimum_fusion
  119.8 51.2 %feed_forward.1 = (bf16[1024,768]{1,0:T(8,128)(2,1)}, f32[1024,768]{1,0:T(8,128)}, bf16[1024,768]{1,0:T(8,128)(2,1)}, bf16[1024,128]{1,0:T(8,128)(2,1)}, bf16[76...) custom-call(bf16[1024,768]{1,0:T(8,128)(2,1)} %bitcast.110, ...), custom_call_target="tpu_custom_call" | custom-call | tf_op jit(solution)/shard_map/feed_forward/pallas_call | solution.py:486
  171.0 0.7 reshape.242
  171.7 1.3 pad_maximum_fusion.early_ref
  173.1 0.0 collective-permute-done.3.qmf_ref
  173.1 0.0 collective-permute-done.2.qf_ref
  173.1 1.2 copy-done.8
  174.3 197.4 %att_bwd.1 = (bf16[1024,768]{1,0:T(8,128)(2,1)}, f32[288,128]{1,0:T(8,128)}, bf16[768,3072]{1,0:T(8,128)(2,1)}, bf16[3072,768]{1,0:T(8,128)(2,1)}, bf16[768,768]{1,0:T(8,128)(2,1)}, /*index=5*/bf16[768,2304]{1,0:T(8,128)(2,1)}) custom-call(bf16[1024,768]{1,0:T(8,128)(2,1)} %copy-done.1, bf16[1024,768]{1,0:T(8,128)(2,1)} %copy-done, ...), custom_call_target="tpu_custom_call" | custom-call | tf_op jit(solution)/shard_map/att_bwd/pallas_call | solution.py:391
  371.7 0.8 slice_bitcast_fusion
  372.5 0.9 slice.151
  373.4 1.3 slice.152
  374.7 0.0 copy-start.16
  374.7 5.6 %bitcast_convert_fusion.2 = f32[1,768,2304]{2,1,0:T(8,128)} fusion(bf16[768,2304]{1,0:T(8,128)(2,1)} %get-tuple-element.46), kind=kLoop, calls=%fused_computation.9 | loop fusion | flops 1769472 | bytes 10616832 | tf_op jit(solution)/shard_map/broadcast_in_dim | solution.py:596
  380.3 0.6 broadcast_in_dim.65
  381.0 0.4 convolution_bitcast_fusion
  381.3 0.1 copy.28
  381.4 0.7 reshape.254
  382.1 1.6 bitcast_convert_fusion.3
  383.7 7.9 %bitcast_convert_fusion.1 = f32[1,768,3072]{2,1,0:T(8,128)} fusion(bf16[768,3072]{1,0:T(8,128)(2,1)} %get-tuple-element.48), kind=kLoop, calls=%fused_computation.4 | loop fusion | flops 2359296 | bytes 14155776 | tf_op jit(solution)/shard_map/broadcast_in_dim | solution.py:596
  391.6 4.5 %bitcast_convert_fusion = f32[1,3072,768]{2,1,0:T(8,128)} fusion(bf16[3072,768]{1,0:T(8,128)(2,1)S(1)} %bitcast.114), kind=kLoop, calls=%fused_computation.3 | loop fusion | flops 2359296 | bytes 14155776 | tf_op jit(solution)/shard_map/broadcast_in_dim | solution.py:596
  396.1 0.6 copy.56
  396.7 0.6 maximum_bitcast_fusion
  397.3 0.6 maximum_bitcast_fusion.1
  397.9 1.1 copy.65
  (46 shorter events, 0.2 us)
Async XLA Ops:
  0.6 4.2 %copy-start.6 = (bf16[1,2,512,768]{3,2,1,0:T(8,128)(2,1)S(1)}, bf16[1,2,512,768]{3,2,1,0:T(8,128)(2,1)}, u32[]{:S(2)}) copy-start(bf16[1,2,512,768]{3,2,1,0:T(8,128)(2,1)} %param.14) | copy-start | bytes 4718596
  0.7 4.1 %copy-start.11 = (f32[1,3,768]{2,0,1:T(1,128)S(1)}, f32[1,3,768]{2,0,1:T(1,128)}, u32[]{:S(2)}) copy-start(f32[1,3,768]{2,0,1:T(1,128)} %param.21) | copy-start | bytes 27652
  0.7 4.1 %copy-start.13 = (f32[1,2,768]{2,1,0:T(2,128)S(1)}, f32[1,2,768]{2,1,0:T(2,128)}, u32[]{:S(2)}) copy-start(f32[1,2,768]{2,1,0:T(2,128)} %param.19) | copy-start | bytes 18436
  0.7 4.1 %copy-start.14 = (f32[1,2,768]{2,1,0:T(2,128)S(1)}, f32[1,2,768]{2,1,0:T(2,128)}, u32[]{:S(2)}) copy-start(f32[1,2,768]{2,1,0:T(2,128)} %param.18) | copy-start | bytes 18436
  0.7 4.8 %copy-start.7 = (bf16[1,768,2304]{2,1,0:T(8,128)(2,1)S(1)}, bf16[1,768,2304]{2,1,0:T(8,128)(2,1)}, u32[]{:S(2)}) copy-start(bf16[1,768,2304]{2,1,0:T(8,128)(2,1)} %param.20) | copy-start | bytes 10616836
  9.7 71.2 %copy-start = (bf16[1024,768]{1,0:T(8,128)(2,1)}, bf16[1024,768]{1,0:T(8,128)(2,1)S(1)}, u32[]{:S(2)}) copy-start(bf16[1024,768]{1,0:T(8,128)(2,1)S(1)} %get-tuple-element.64.kn_ref) | copy-start | bytes 4718596
  9.8 105.1 %copy-start.1 = (bf16[1024,768]{1,0:T(8,128)(2,1)}, bf16[1024,768]{1,0:T(8,128)(2,1)S(1)}, u32[]{:S(2)}) copy-start(bf16[1024,768]{1,0:T(8,128)(2,1)S(1)} %get-tuple-element.36.q_ref) | copy-start | bytes 4718596
  9.8 5.0 %copy-start.15 = (f32[1,64,12]{1,0,2:T(1,128)S(1)}, f32[1,64,12]{1,0,2:T(1,128)}, u32[]{:S(2)}) copy-start(f32[1,64,12]{1,0,2:T(1,128)} %param.22) | copy-start | bytes 9220
  9.8 38.3 %collective-permute-start = (bf16[1024,768]{1,0:T(8,128)(2,1)S(1)}, bf16[1024,768]{1,0:T(8,128)(2,1)}, u32[]{:S(2)}, u32[]{:S(2)}) collective-permute-start(bf16[1024,768]{1,0:T(8,128)(2,1)S(1)} %get-tuple-element.64.kn_ref), channel_id=1, source_target_pairs={{0,16},{16,0},{1,17},{17,1},{2,18},{18,2},{3,19},{19,3},{4,20},{20... | collective-permute-start | bytes 4718600 | tf_op jit(solution)/shard_map/ppermute | solution.py:501
  14.2 66.8 %collective-permute-start.1 = (bf16[1024,768]{1,0:T(8,128)(2,1)}, bf16[1024,768]{1,0:T(8,128)(2,1)}, u32[]{:S(2)}, u32[]{:S(2)}) collective-permute-start(bf16[1024,768]{1,0:T(8,128)(2,1)} %fusion.7.vn_ref), channel_id=1, source_target_pairs={{0,16},{16,0},{1,17},{17,1},{2,18},{18,2},{3,19},{19,3},{4,20},{20... | collective-permute-start | bytes 4718600 | tf_op jit(solution)/shard_map/ppermute | solution.py:501
  17.4 1.7 copy-start.17
  17.4 1.8 copy-start.12
  19.6 94.1 %copy-start.3 = (bf16[1024,128]{1,0:T(8,128)(2,1)}, bf16[1024,128]{1,0:T(8,128)(2,1)S(1)}, u32[]{:S(2)}) copy-start(bf16[1024,128]{1,0:T(8,128)(2,1)S(1)} %select_convert_fusion.kseg_ref) | copy-start | bytes 786436
  19.8 93.9 %copy-start.2 = (bf16[1024,256]{1,0:T(8,128)(2,1)}, bf16[1024,256]{1,0:T(8,128)(2,1)S(1)}, u32[]{:S(2)}) copy-start(bf16[1024,256]{1,0:T(8,128)(2,1)S(1)} %fusion.10.e_ref) | copy-start | bytes 1572868
  81.0 37.5 %copy-start.18 = (f32[1,768]{1,0:T(1,128)S(1)}, f32[1,768]{1,0:T(1,128)}, u32[]{:S(2)}) copy-start(f32[1,768]{1,0:T(1,128)} %param.27) | copy-start | bytes 9220
  113.7 1.2 copy-start.4
  114.8 56.2 %copy-start.5 = (bf16[1024,128]{1,0:T(8,128)(2,1)}, bf16[1024,128]{1,0:T(8,128)(2,1)S(1)}, u32[]{:S(2)}) copy-start(bf16[1024,128]{1,0:T(8,128)(2,1)S(1)} %get-tuple-element.37.qm_ref) | copy-start | bytes 786436
  114.8 58.2 %collective-permute-start.2 = (bf16[1024,768]{1,0:T(8,128)(2,1)S(1)}, bf16[1024,768]{1,0:T(8,128)(2,1)S(1)}, u32[]{:S(2)}, u32[]{:S(2)}) collective-permute-start(bf16[1024,768]{1,0:T(8,128)(2,1)S(1)} %get-tuple-element.36.q_ref), channel_id=1, source_target_pairs={{0,16},{16,0},{1,17},{17,1},{2,18},{18,2},{3,19},{19,3},{4,20},{20... | collective-permute-start | bytes 4718600 | tf_op jit(solution)/shard_map/ppermute | solution.py:501
  118.2 54.8 %collective-permute-start.3 = (bf16[1024,128]{1,0:T(8,128)(2,1)S(1)}, bf16[1024,128]{1,0:T(8,128)(2,1)}, u32[]{:S(2)}, u32[]{:S(2)}) collective-permute-start(bf16[1024,128]{1,0:T(8,128)(2,1)S(1)} %get-tuple-element.37.qm_ref), channel_id=1, source_target_pairs={{0,16},{16,0},{1,17},{17,1},{2,18},{18,2},{3,19},{19,3},{4,20},{20... | collective-permute-start | bytes 786440 | tf_op jit(solution)/shard_map/ppermute | solution.py:501
  173.1 1.2 copy-start.8
  374.7 6.2 %copy-start.16 = (s32[2,16]{1,0:T(2,128)S(1)}, s32[2,16]{1,0:T(2,128)}, u32[]{:S(2)}) copy-start(s32[2,16]{1,0:T(2,128)} %add_minimum_fusion) | copy-start | bytes 388
  374.7 7.4 %copy-start.10 = (bf16[768,768]{1,0:T(8,128)(2,1)S(1)}, bf16[768,768]{1,0:T(8,128)(2,1)}, u32[]{:S(2)}) copy-start(bf16[768,768]{1,0:T(8,128)(2,1)} %get-tuple-element.47) | copy-start | bytes 3538948
  382.1 9.5 %slice-start = ((s8[4718592]{0:T(1024)(128)(4,1)}), s8[4194304]{0:T(1024)(128)(4,1)S(1)}, s32[]{:S(2)}) async-start(s8[4718592]{0:T(1024)(128)(4,1)} %bitcast.113), calls=%async_computation | async-start | bytes 8388608
  383.7 7.9 %slice-start.1 = ((s8[4718592]{0:T(1024)(128)(4,1)}), s8[524288]{0:T(1024)(128)(4,1)S(1)}, s32[]{:S(2)}) async-start(s8[4718592]{0:T(1024)(128)(4,1)} %bitcast.113), calls=%async_computation.1 | async-start | bytes 1048576
  391.6 6.3 %copy-start.9 = (bf16[1024,768]{1,0:T(8,128)(2,1)S(1)}, bf16[1024,768]{1,0:T(8,128)(2,1)}, u32[]{:S(2)}) copy-start(bf16[1024,768]{1,0:T(8,128)(2,1)} %get-tuple-element.44) | copy-start | bytes 4718596

commit v2 on v1

--- a/solution.py
+++ b/solution.py
@@ -17,51 +17,6 @@
 def three(x):
     hi=x.astype(BF); r=x-hi.astype(jnp.float32); mid=r.astype(BF); lo=(r-mid.astype(jnp.float32)).astype(BF)
     return hi,mid,lo
-
-def fwd_kernel(CQ, q_ref,kn_ref,kf_ref,vn_ref,vf_ref,e_ref,b_ref,qseg_ref,kseg_ref,o_ref,qm_ref):
-    pair=pl.program_id(1)
-    L=q_ref.shape[0]
-    lane=lax.broadcasted_iota(jnp.int32,(1,128),1)
-    @pl.when(pair==0)
-    def _():
-        qm_ref[...]=qseg_ref[...]
-    outs=[None]*(L//CQ)
-    for hh in range(2):
-        mh=(lane<64) if hh==0 else (lane>=64)
-        h=2*pair+hh
-        C=mm(e_ref[...],b_ref[hh]).astype(BF)
-        kx=jnp.concatenate([kn_ref[...],C,kseg_ref[...]],axis=1)
-        kf=kf_ref[...]
-        one=jnp.ones((),BF); zero=jnp.zeros((),BF)
-        vnx=jnp.where(mh,vn_ref[...],one); vfx=jnp.where(mh,vf_ref[...],one)
-        for c in range(L//CQ):
-            sl=slice(c*CQ,(c+1)*CQ)
-            qm=jnp.where(mh,q_ref[sl,:],zero)
-            qx=jnp.concatenate([qm,e_ref[sl,:],qseg_ref[sl,:]],axis=1)
-            sn=mm(qx,kx,NT); sf=mm(qm,kf,NT)
-            m=jnp.maximum(jnp.max(sn,axis=1,keepdims=True),jnp.max(sf,axis=1,keepdims=True))
-            pn=jnp.exp(sn-m).astype(BF); pf=jnp.exp(sf-m).astype(BF)
-            o=mm(pn,vnx)+mm(pf,vfx)
-            l=pltpu.roll(o,64,1)
-            on=o/l
-            outs[c]=on if hh==0 else jnp.where(mh,on,outs[c])
-            lse=-(m+jnp.log(jnp.where(mh,l,o)))
-            hi,mid,lo=three(lse)
-            cur=qm_ref[sl,:]
-            cur=jnp.where(lane==3*h,hi,cur); cur=jnp.where(lane==3*h+1,mid,cur); cur=jnp.where(lane==3*h+2,lo,cur)
-            qm_ref[sl,:]=cur
-    for c in range(L//CQ):
-        o_ref[c*CQ:(c+1)*CQ,:]=outs[c].astype(BF)
-
-def fwd(q,kn,kf,vn,vf,e,bt,qseg,kseg,L,CQ=512):
-    T=q.shape[0]; R=T//L; NP=q.shape[1]//128
-    blk=pl.BlockSpec((L,128),lambda r,p:(r,p))
-    row=lambda w: pl.BlockSpec((L,w),lambda r,p:(r,0))
-    return pl.pallas_call(functools.partial(fwd_kernel,CQ),grid=(R,NP),
-        in_specs=[blk]*5+[row(256),pl.BlockSpec((2,256,256),lambda r,p:(p,0,0)),row(128),row(128)],
-        out_specs=[blk,row(128)],
-        out_shape=[jax.ShapeDtypeStruct(q.shape,BF),jax.ShapeDtypeStruct((T,128),BF)],
-        compiler_params=pltpu.CompilerParams(vmem_limit_bytes=48<<20),name="att_fwd")(q,kn,kf,vn,vf,e,bt,qseg,kseg)
 
 
 F32=jnp.float32
@@ -402,6 +357,143 @@
         name="att_bwd")(q,kn,kf,vn,vf,do,dm,qmisc,e,et,bt,kseg,qf,qmf,feat,wqkv,gm,vec,early,do,dm,*grads)
 
 
+def front_kernel(NP, R, q_ref, kn_ref, vn_ref, e_ref, b_ref, qseg_ref, kseg_ref, k_any, v_any,
+                 o_ref, kf_ref, vf_ref, qm_ref, kfs, vfs, onear, mnear, ks, kr, vs, vr):
+    step = pl.program_id(0)
+    per = NP * R
+    inner = step % per
+    pair = inner // R
+    r = inner % R
+    L = q_ref.shape[0]
+    other = {"stream": 1 - lax.axis_index("stream")}
+    lane = lax.broadcasted_iota(jnp.int32, (1, 128), 1)
+    zero = jnp.zeros((), BF)
+    one = jnp.ones((), BF)
+    at = pl.ds(pl.multiple_of(r * L, L), L)
+
+    def copies(p):
+        cols = pl.ds(p * 128, 128)
+        return (pltpu.make_async_remote_copy(k_any.at[:, cols], kfs.at[p], ks.at[p], kr.at[p], device_id=other, device_id_type=MESH),
+                pltpu.make_async_remote_copy(v_any.at[:, cols], vfs.at[p], vs.at[p], vr.at[p], device_id=other, device_id_type=MESH))
+
+    @pl.when(step == 0)
+    def _():
+        sem = pltpu.get_barrier_semaphore()
+        pl.semaphore_signal(sem, inc=1, device_id=other, device_id_type=MESH)
+        pl.semaphore_wait(sem, 1)
+        for p in range(2):
+            for d in copies(p):
+                d.start()
+        qm_ref[...] = qseg_ref[...]
+
+    @pl.when(step == 2 * per // 3)
+    def _():
+        for d in copies(0):
+            d.wait_send()
+        for d in copies(2):
+            d.start()
+
+    for p in range(NP):
+        @pl.when(step == per + p * R)
+        def _():
+            for d in copies(p):
+                d.wait_recv()
+            if p > 0:
+                for d in copies(p):
+                    d.wait_send()
+                if p + 2 < NP:
+                    for d in copies(p + 2):
+                        d.start()
+
+    def half_of(hh):
+        return (lane < 64) if hh == 0 else (lane >= 64)
+
+    @pl.when(step < per)
+    def _():
+        for hh in range(2):
+            mh = half_of(hh)
+            table = mm(e_ref[...], b_ref[hh]).astype(BF)
+            kx = jnp.concatenate([kn_ref[...], table, kseg_ref[at, :]], axis=1)
+            qx = jnp.concatenate([jnp.where(mh, q_ref[...], zero), e_ref[...], qseg_ref[at, :]], axis=1)
+            s = mm(qx, kx, NT)
+            m = jnp.max(s, axis=1, keepdims=True)
+            p = jnp.exp(s - m).astype(BF)
+            onear[inner, hh] = mm(p, jnp.where(mh, vn_ref[...], one))
+            mnear[inner, hh] = jnp.broadcast_to(m, (L, 128))
+
+    @pl.when(step >= per)
+    def _():
+        out = None
+        kf = kfs[pair, at]
+        vf = vfs[pair, at]
+        kf_ref[...] = kf
+        vf_ref[...] = vf
+        for hh in range(2):
+            mh = half_of(hh)
+            h = 2 * pair + hh
+            s = mm(jnp.where(mh, q_ref[...], zero), kf, NT)
+            before = mnear[inner, hh]
+            m = jnp.maximum(before, jnp.max(s, axis=1, keepdims=True))
+            p = jnp.exp(s - m[:, :1]).astype(BF)
+            o = mm(p, jnp.where(mh, vf, one)) + jnp.exp(before - m) * onear[inner, hh]
+            l = pltpu.roll(o, 64, 1)
+            on = o / l
+            out = on if hh == 0 else jnp.where(mh, on, out)
+            hi, mid_part, lo = three(-(m + jnp.log(jnp.where(mh, l, o))))
+            cur = qm_ref[at, :]
+            cur = jnp.where(lane == 3 * h, hi, cur)
+            cur = jnp.where(lane == 3 * h + 1, mid_part, cur)
+            qm_ref[at, :] = jnp.where(lane == 3 * h + 2, lo, cur)
+        o_ref[...] = out.astype(BF)
+
+
+def front(q, k, v, e, bt, qseg, kseg, L, collective_id):
+    T, D = q.shape
+    R, NP = T // L, D // 128
+    per = R * NP
+
+    def cyc(s):
+        return (s % per) % R, (s % per) // R
+
+    def one(s):
+        i = jnp.minimum(s, per - 1)
+        return i % R, i // R
+
+    def two(s):
+        i = jnp.maximum(s - per, 0)
+        return i % R, i // R
+
+    blk = lambda f: pl.BlockSpec((L, 128), f)
+    full = lambda a: pl.BlockSpec(a.shape, lambda s: (0,) * len(a.shape), pipeline_mode=pl.Buffered(1))
+    any_ = pl.BlockSpec(memory_space=pl.ANY)
+    S = jax.ShapeDtypeStruct
+    sem = pltpu.SemaphoreType.DMA((NP,))
+    return pl.pallas_call(
+        functools.partial(front_kernel, NP, R), grid=(2 * per,),
+        in_specs=[blk(cyc), blk(one), blk(one), pl.BlockSpec((L, 256), lambda s: (one(s)[0], 0)),
+                  pl.BlockSpec((2, 256, 256), lambda s: (one(s)[1], 0, 0)), full(qseg), full(kseg), any_, any_],
+        out_specs=[blk(two)] * 3 + [full(qseg)],
+        out_shape=[S((T, D), BF)] * 3 + [S((T, 128), BF)],
+        scratch_shapes=[pltpu.VMEM((NP, T, 128), BF), pltpu.VMEM((NP, T, 128), BF),
+                        pltpu.VMEM((per, 2, L, 128), F32), pltpu.VMEM((per, 2, L, 128), F32), sem, sem, sem, sem],
+        compiler_params=pltpu.CompilerParams(collective_id=collective_id, has_side_effects=True, vmem_limit_bytes=60 << 20),
+        name="att_fwd")(q, k, v, e, bt, qseg, kseg, k, v)
+
+
+def widen_kernel(*refs):
+    half = len(refs) // 2
+    for i in range(half):
+        refs[half + i][...] = refs[i][...].astype(F32)
+
+
+def widen(arrays, parts=16):
+    spec = lambda a: pl.BlockSpec((a.shape[0] // parts, a.shape[1]), lambda i: (i, 0))
+    return pl.pallas_call(
+        widen_kernel, grid=(parts,), in_specs=[spec(a) for a in arrays], out_specs=[spec(a) for a in arrays],
+        out_shape=[jax.ShapeDtypeStruct(a.shape, F32) for a in arrays],
+        compiler_params=pltpu.CompilerParams(vmem_limit_bytes=32 << 20), name="widen")(*arrays)
+
+
 def gelu_both(u):
     a=jnp.abs(u)
     t=1.0/(1.0+a*(0.3275911*0.7071067811865476))
@@ -556,12 +648,10 @@
     queries = (combined[:, :width] + bias_rows[0]).astype(BF) * BF(0.125)
     key_part = combined[:, width:2 * width].astype(BF)
     value_part = (combined[:, 2 * width:] + bias_rows[1]).astype(BF)
-    partner_k = from_partner(key_part, "stream", 0)
-    partner_v = from_partner(value_part, "stream", 0)
     e, et, qseg, kseg = prepare(segment_ids, box_cells[0], distance_table[0], is_vision)
     onehot = code_onehot()
     bt = jnp.dot(distance_table[0].T.astype(BF), onehot, preferred_element_type=jnp.float32).astype(BF).reshape(heads, 256, 256)
-    attended, qmisc = fwd(queries, key_part, partner_k, value_part, partner_v, e, bt, qseg, kseg, length)
+    attended, partner_k, partner_v, qmisc = front(queries, key_part, value_part, e, bt, qseg, kseg, length, 6)
     vec = jnp.concatenate([bias_rows[2:3], norm_gains[1:2], norm_shifts[1:2], down_bias, jnp.zeros((4, width), F32)])
     q_send, m_send = lax.optimization_barrier((queries, qmisc))
     partner_q = from_partner(q_send, "stream", 0)
@@ -593,7 +683,8 @@
     shift = jnp.stack([last[1], mid_sums[1]])[None]
     bias = jnp.stack([last[2], last[3], mid_sums[2]])[None]
     downb = mid_sums[3][None]
-    f32 = lambda a: a.astype(jnp.float32)[None]
+    sum_qkv, sum_out, sum_up, sum_down = widen([sum_qkv, sum_out, sum_up, sum_down])
+    f32 = lambda a: a[None]
     return (output, input_grad, gain, shift, f32(sum_qkv), bias, dist, f32(sum_out), f32(sum_up), upb, f32(sum_down), downb)
 
 

time: 402 us -> 390 us (0.970); the launches traced: 399 us -> 383 us
  waiting for transfers between devices: 61.2 us -> 0.01 us
  Pallas kernels: 281 us -> 338 us
  other arithmetic: 31.5 us -> 15.8 us
  local copies, waits for them, and re-layouts: 11.9 us -> 18.6 us
    ppermute x4 -> x2, waiting for transfers between devices: 61.2 us -> 0.01 us  [from_partner(): return lax.ppermute(block, axis, route)]
    pallas_call x1 -> x2, Pallas kernels: 32.6 us -> 88.3 us  [the longest x1 77.8 us: front(): pl.pallas_call(functools.partial(front_kernel, NP, R), grid=(2 * per,), i...]
    broadcast_in_dim x4 -> x0, other arithmetic: 19.5 us -> none  [on_device(): f32 = lambda a: a.astype(jnp.float32)[None]]
    unnamed x54 -> x46, local copies, waits for them, and re-layouts: 5.5 us -> 12.2 us
  transfers between devices with their start and end apart: 4 -> 2, of which waited for: 2 -> 0; matrix products, arithmetic and copies ran while one was open for 3% -> 1% of each run, Pallas kernels for 13% -> 13%
where the time goes in v2:
time: 390 us; the launch traced here: 383 us
  Pallas kernels  338 us (87%)
  local copies, waits for them, and re-layouts  18.6 us (5%)
  other arithmetic  15.8 us (4%)
  matrix products  7.47 us (2%)
    pallas_call x1, Pallas kernels, back(): pl.pallas_call(functools.partial(back_kernel, n, NP, R, chunks, loads, cu...  198 us
    pallas_call x1, Pallas kernels, front(): pl.pallas_call(functools.partial(front_kernel, NP, R), grid=(2 * per,), i...  77.8 us
    pallas_call x1, Pallas kernels, mid(): pl.pallas_call(functools.partial(mid_kernel, RC), grid=(FF // FT,), in_sp...  51 us
    unnamed x46, local copies, waits for them, and re-layouts  12.2 us
    pallas_call x1, Pallas kernels, widen(): pl.pallas_call(widen_kernel, grid=(parts,), in_specs=[spec(a) for a in ar...  10.6 us
  transfers between devices with their start and end apart: 2, of which 0 were waited for; matrix products, arithmetic and copies ran while one was open for 1% of the time, Pallas kernels for 13%

profile of v2, /device:TPU:0, one launch (start us, length us, event | category | flops | bytes accessed | tf_op | source)
XLA Modules:
  0.0 382.7 jit_solution(4532608917812328060)
XLA Ops:
  0.6 0.0 copy-start.4
  0.7 0.0 copy-start.10
  0.7 0.0 copy-start.12
  0.7 0.0 copy-start.13
  0.7 0.2 fusion.24
  0.9 0.0 copy-start.6
  0.9 1.9 convert_reduce_fusion
  2.8 2.0 fusion.3
  4.8 0.0 copy-done.10
  4.8 0.0 copy-done.12
  4.9 0.0 copy-done.13
  4.9 0.0 copy-done.4
  4.9 0.6 fusion.6
  5.5 0.0 copy-done.6
  5.6 3.8 %fusion.41 = f32[1024,2304]{1,0:T(8,128)S(1)} fusion(bf16[1024,768]{1,0:T(8,128)(2,1)S(1)} %bitcast.111, bf16[1,768,2304]{2,1,0:T(8,128)(2,1)S(1)} %copy-done.6), kind=kOutput, calls=%fused_computation.108 | convolution fusion | flops 3623878656 | bytes 14548992 | tf_op jit(solution)/shard_map/dot_general | solution.py:647
  9.4 2.1 fusion.43
  11.5 0.0 copy-start.11
  11.5 0.0 copy-start.14
  11.5 1.4 fusion.7.vn_ref.v_any
  12.9 0.0 copy-done.11
  13.0 1.0 fusion.10.e_ref
  14.0 0.0 copy-done.14
  14.0 2.6 convolution_convert_fusion
  16.6 0.5 copy.32
  17.1 1.3 slice.160.b_ref
  18.4 0.0 copy-done.15
  18.4 0.9 compare_convert_fusion.qseg_ref
  19.3 0.9 select_convert_fusion.kseg_ref
  20.2 77.8 %att_fwd.1 = (bf16[1024,768]{1,0:T(8,128)(2,1)}, bf16[1024,768]{1,0:T(8,128)(2,1)}, bf16[1024,768]{1,0:T(8,128)(2,1)}, bf16[1024,128]{1,0:T(8,128)(2,1)}) custom-call(bf16[1024,768]{1,0:T(8,128)(2,1)} %get-tuple-element.44.q_ref, bf16[1024,768]{1,0:T(8,128)(2,1)} %get-tuple-element.76.kn_ref.k_any, bf16[1024,768]{1,0:T(8,128)(2,1)} %fusion.7.vn_ref.v_any, ...), custom_call_target="tpu_custom_call" | custom-call | tf_op jit(solution)/shard_map/att_fwd/pallas_call | solution.py:471
  98.0 0.0 copy-done.5
  98.0 1.8 collective-permute-start
  99.8 0.3 collective-permute-start.1
  100.1 0.0 copy-done.16
  100.1 0.6 concatenate.13.vec_ref
  100.7 51.0 %feed_forward.1 = (bf16[1024,768]{1,0:T(8,128)(2,1)}, f32[1024,768]{1,0:T(8,128)}, bf16[1024,768]{1,0:T(8,128)(2,1)}, bf16[1024,128]{1,0:T(8,128)(2,1)}, bf16[76...) custom-call(bf16[1024,768]{1,0:T(8,128)(2,1)} %bitcast.102, ...), custom_call_target="tpu_custom_call" | custom-call | tf_op jit(solution)/shard_map/feed_forward/pallas_call | solution.py:578
  151.7 0.7 reshape.242
  152.4 0.1 pad.13.clone
  152.5 1.3 pad_maximum_fusion.early_ref
  153.8 0.7 maximum_maximum_fusion.vec_ref
  154.5 0.6 add_minimum_fusion
  155.1 0.9 fusion.11.et_ref
  156.0 0.0 collective-permute-done.1.qmf_ref
  156.0 0.0 collective-permute-done.qf_ref
  156.0 0.0 copy-start.7
  156.0 1.2 copy-done.7
  157.2 0.0 copy-done.9
  157.3 198.3 %att_bwd.1 = (bf16[1024,768]{1,0:T(8,128)(2,1)}, f32[288,128]{1,0:T(8,128)}, bf16[768,3072]{1,0:T(8,128)(2,1)}, bf16[3072,768]{1,0:T(8,128)(2,1)}, bf16[768,768]{1,0:T(8,128)(2,1)}, /*index=5*/bf16[768,2304]{1,0:T(8,128)(2,1)}) custom-call(bf16[1024,768]{1,0:T(8,128)(2,1)} %get-tuple-element.44.q_ref, bf16[1024,768]{1,0:T(8,128)(2,1)} %get-tuple-element.76.kn_ref.k_any, ...), custom_call_target="tpu_custom_call" | custom-call | tf_op jit(solution)/shard_map/att_bwd/pallas_call | solution.py:346
  355.5 0.8 slice_bitcast_fusion
  356.3 0.9 slice.151
  357.2 1.3 slice.152
  358.6 0.6 broadcast_in_dim.52
  359.2 1.0 convolution_bitcast_fusion
  360.2 0.1 copy.28
  360.4 0.7 reshape.250
  361.1 0.6 copy.56
  361.7 0.6 maximum_bitcast_fusion
  362.3 0.6 maximum_bitcast_fusion.1
  362.9 2.3 copy-done
  365.2 2.3 copy-done.1
  367.5 2.0 copy-done.2
  369.5 1.3 copy-done.3
  370.8 10.6 %widen.1 = (f32[768,2304]{1,0:T(8,128)}, f32[768,768]{1,0:T(8,128)}, f32[768,3072]{1,0:T(8,128)}, f32[3072,768]{1,0:T(8,128)}) custom-call(bf16[768,2304]{1,0:T(8,128)(2,1)S(1)} %copy-done.2, bf16[768,768]{1,0:T(8,128)(2,1)S(1)} %copy-done.3, bf16[768,3072]{1,0:T(8,128)(2,1)S(1)} %copy-done, bf16[3072,768]{1,0:T(8,128)(2,1)S(1)} %copy-done.1), custom_call_target="tpu_custom_call" | custom-call | tf_op jit(solution)/shard_map/widen/pallas_call | solution.py:491
  381.4 0.0 copy-done.8
  381.4 1.1 copy.65
  (30 shorter events, 0.2 us)
Async XLA Ops:
  0.6 4.3 %copy-start.4 = (bf16[1,2,512,768]{3,2,1,0:T(8,128)(2,1)S(1)}, bf16[1,2,512,768]{3,2,1,0:T(8,128)(2,1)}, u32[]{:S(2)}) copy-start(bf16[1,2,512,768]{3,2,1,0:T(8,128)(2,1)} %param.14) | copy-start | bytes 4718596
  0.7 4.2 %copy-start.10 = (f32[1,3,768]{2,0,1:T(1,128)S(1)}, f32[1,3,768]{2,0,1:T(1,128)}, u32[]{:S(2)}) copy-start(f32[1,3,768]{2,0,1:T(1,128)} %param.21) | copy-start | bytes 27652
  0.7 4.2 %copy-start.12 = (f32[1,2,768]{2,1,0:T(2,128)S(1)}, f32[1,2,768]{2,1,0:T(2,128)}, u32[]{:S(2)}) copy-start(f32[1,2,768]{2,1,0:T(2,128)} %param.19) | copy-start | bytes 18436
  0.7 4.2 %copy-start.13 = (f32[1,2,768]{2,1,0:T(2,128)S(1)}, f32[1,2,768]{2,1,0:T(2,128)}, u32[]{:S(2)}) copy-start(f32[1,2,768]{2,1,0:T(2,128)} %param.18) | copy-start | bytes 18436
  0.9 4.7 %copy-start.6 = (bf16[1,768,2304]{2,1,0:T(8,128)(2,1)S(1)}, bf16[1,768,2304]{2,1,0:T(8,128)(2,1)}, u32[]{:S(2)}) copy-start(bf16[1,768,2304]{2,1,0:T(8,128)(2,1)} %param.20) | copy-start | bytes 10616836
  11.5 1.4 copy-start.11
  11.5 2.4 copy-start.14
  16.6 1.8 copy-start.15
  20.2 77.8 %copy-start.5 = (bf16[1024,768]{1,0:T(8,128)(2,1)S(1)}, bf16[1024,768]{1,0:T(8,128)(2,1)}, u32[]{:S(2)}) copy-start(bf16[1024,768]{1,0:T(8,128)(2,1)} %get-tuple-element.44.q_ref) | copy-start | bytes 4718596
  20.2 79.9 %copy-start.16 = (f32[1,768]{1,0:T(1,128)S(1)}, f32[1,768]{1,0:T(1,128)}, u32[]{:S(2)}) copy-start(f32[1,768]{1,0:T(1,128)} %param.27) | copy-start | bytes 9220
  98.0 58.1 %collective-permute-start = (bf16[1024,768]{1,0:T(8,128)(2,1)S(1)}, bf16[1024,768]{1,0:T(8,128)(2,1)S(1)}, u32[]{:S(2)}, u32[]{:S(2)}) collective-permute-start(bf16[1024,768]{1,0:T(8,128)(2,1)S(1)} %copy-done.5), channel_id=1, source_target_pairs={{0,16},{16,0},{1,17},{17,1},{2,18},{18,2},{3,19},{19,3},{4,20},{20... | collective-permute-start | bytes 4718600 | tf_op jit(solution)/shard_map/ppermute | solution.py:593
  99.8 56.2 %collective-permute-start.1 = (bf16[1024,128]{1,0:T(8,128)(2,1)}, bf16[1024,128]{1,0:T(8,128)(2,1)S(1)}, u32[]{:S(2)}, u32[]{:S(2)}) collective-permute-start(bf16[1024,128]{1,0:T(8,128)(2,1)} %get-tuple-element.45.qm_ref), channel_id=1, source_target_pairs={{0,16},{16,0},{1,17},{17,1},{2,18},{18,2},{3,19},{19,3},{4,20},{20... | collective-permute-start | bytes 786440 | tf_op jit(solution)/shard_map/ppermute | solution.py:593
  156.0 1.2 copy-start.9
  156.0 1.2 copy-start.7
  362.9 2.3 copy-start
  365.2 2.3 copy-start.1
  367.5 2.0 copy-start.2
  369.5 1.3 copy-start.3
  370.8 10.6 %copy-start.8 = (bf16[1024,768]{1,0:T(8,128)(2,1)S(1)}, bf16[1024,768]{1,0:T(8,128)(2,1)}, u32[]{:S(2)}) copy-start(bf16[1024,768]{1,0:T(8,128)(2,1)} %get-tuple-element.52) | copy-start | bytes 4718596

commit v3 on v2

--- a/solution.py
+++ b/solution.py
@@ -357,14 +357,17 @@
         name="att_bwd")(q,kn,kf,vn,vf,do,dm,qmisc,e,et,bt,kseg,qf,qmf,feat,wqkv,gm,vec,early,do,dm,*grads)
 
 
-def front_kernel(NP, R, q_ref, kn_ref, vn_ref, e_ref, b_ref, qseg_ref, kseg_ref, k_any, v_any,
-                 o_ref, kf_ref, vf_ref, qm_ref, kfs, vfs, onear, mnear, ks, kr, vs, vr):
+def front_kernel(NP, R, feat_ref, w_ref, vec_ref, e_ref, b_ref, qseg_ref, kseg_ref,
+                 o_ref, kf_ref, vf_ref, qm_ref, q_s, k_s, v_s, nrm_s, kfs, vfs, onear, mnear, ks, kr, vs, vr):
     step = pl.program_id(0)
     per = NP * R
     inner = step % per
     pair = inner // R
     r = inner % R
-    L = q_ref.shape[0]
+    L = e_ref.shape[0]
+    T, D = feat_ref.shape
+    GROUP = 256
+    mine = pl.ds(pl.multiple_of(pair * 128, 128), 128)
     other = {"stream": 1 - lax.axis_index("stream")}
     lane = lax.broadcasted_iota(jnp.int32, (1, 128), 1)
     zero = jnp.zeros((), BF)
@@ -373,17 +376,29 @@
 
     def copies(p):
         cols = pl.ds(p * 128, 128)
-        return (pltpu.make_async_remote_copy(k_any.at[:, cols], kfs.at[p], ks.at[p], kr.at[p], device_id=other, device_id_type=MESH),
-                pltpu.make_async_remote_copy(v_any.at[:, cols], vfs.at[p], vs.at[p], vr.at[p], device_id=other, device_id_type=MESH))
+        return (pltpu.make_async_remote_copy(k_s.at[:, cols], kfs.at[p], ks.at[p], kr.at[p], device_id=other, device_id_type=MESH),
+                pltpu.make_async_remote_copy(v_s.at[:, cols], vfs.at[p], vs.at[p], vr.at[p], device_id=other, device_id_type=MESH))
 
     @pl.when(step == 0)
     def _():
         sem = pltpu.get_barrier_semaphore()
         pl.semaphore_signal(sem, inc=1, device_id=other, device_id_type=MESH)
-        pl.semaphore_wait(sem, 1)
-        for p in range(2):
-            for d in copies(p):
-                d.start()
+        for i in range(T // GROUP):
+            sl = slice(i * GROUP, (i + 1) * GROUP)
+            nrm, _ = norm_parts(feat_ref[sl, :].astype(F32))
+            nrm_s[sl, :] = (nrm * vec_ref[0:1, :] + vec_ref[1:2, :]).astype(BF)
+        for g in range(D // GROUP):
+            sl = slice(g * GROUP, (g + 1) * GROUP)
+            k_s[:, sl] = mm(nrm_s[...], w_ref[:, D + g * GROUP:D + (g + 1) * GROUP]).astype(BF)
+            v_s[:, sl] = (mm(nrm_s[...], w_ref[:, 2 * D + g * GROUP:2 * D + (g + 1) * GROUP]) + vec_ref[3:4, sl]).astype(BF)
+            if g == 0:
+                pl.semaphore_wait(sem, 1)
+                for p in range(2):
+                    for d in copies(p):
+                        d.start()
+        for g in range(D // GROUP):
+            sl = slice(g * GROUP, (g + 1) * GROUP)
+            q_s[:, sl] = (mm(nrm_s[...], w_ref[:, sl]) + vec_ref[2:3, sl]).astype(BF) * BF(0.125)
         qm_ref[...] = qseg_ref[...]
 
     @pl.when(step == 2 * per // 3)
@@ -413,12 +428,12 @@
         for hh in range(2):
             mh = half_of(hh)
             table = mm(e_ref[...], b_ref[hh]).astype(BF)
-            kx = jnp.concatenate([kn_ref[...], table, kseg_ref[at, :]], axis=1)
-            qx = jnp.concatenate([jnp.where(mh, q_ref[...], zero), e_ref[...], qseg_ref[at, :]], axis=1)
+            kx = jnp.concatenate([k_s[at, mine], table, kseg_ref[at, :]], axis=1)
+            qx = jnp.concatenate([jnp.where(mh, q_s[at, mine], zero), e_ref[...], qseg_ref[at, :]], axis=1)
             s = mm(qx, kx, NT)
             m = jnp.max(s, axis=1, keepdims=True)
             p = jnp.exp(s - m).astype(BF)
-            onear[inner, hh] = mm(p, jnp.where(mh, vn_ref[...], one))
+            onear[inner, hh] = mm(p, jnp.where(mh, v_s[at, mine], one))
             mnear[inner, hh] = jnp.broadcast_to(m, (L, 128))
 
     @pl.when(step >= per)
@@ -431,7 +446,7 @@
         for hh in range(2):
             mh = half_of(hh)
             h = 2 * pair + hh
-            s = mm(jnp.where(mh, q_ref[...], zero), kf, NT)
+            s = mm(jnp.where(mh, q_s[at, mine], zero), kf, NT)
             before = mnear[inner, hh]
             m = jnp.maximum(before, jnp.max(s, axis=1, keepdims=True))
             p = jnp.exp(s - m[:, :1]).astype(BF)
@@ -447,13 +462,10 @@
         o_ref[...] = out.astype(BF)
 
 
-def front(q, k, v, e, bt, qseg, kseg, L, collective_id):
-    T, D = q.shape
+def front(feat, w, vec, e, bt, qseg, kseg, L, collective_id):
+    T, D = feat.shape
     R, NP = T // L, D // 128
     per = R * NP
-
-    def cyc(s):
-        return (s % per) % R, (s % per) // R
 
     def one(s):
         i = jnp.minimum(s, per - 1)
@@ -470,14 +482,14 @@
     sem = pltpu.SemaphoreType.DMA((NP,))
     return pl.pallas_call(
         functools.partial(front_kernel, NP, R), grid=(2 * per,),
-        in_specs=[blk(cyc), blk(one), blk(one), pl.BlockSpec((L, 256), lambda s: (one(s)[0], 0)),
-                  pl.BlockSpec((2, 256, 256), lambda s: (one(s)[1], 0, 0)), full(qseg), full(kseg), any_, any_],
-        out_specs=[blk(two)] * 3 + [full(qseg)],
-        out_shape=[S((T, D), BF)] * 3 + [S((T, 128), BF)],
-        scratch_shapes=[pltpu.VMEM((NP, T, 128), BF), pltpu.VMEM((NP, T, 128), BF),
+        in_specs=[full(feat), full(w), full(vec), pl.BlockSpec((L, 256), lambda s: (one(s)[0], 0)),
+                  pl.BlockSpec((2, 256, 256), lambda s: (one(s)[1], 0, 0)), full(qseg), full(kseg)],
+        out_specs=[blk(two)] * 3 + [full(qseg)] + [full(feat)] * 3,
+        out_shape=[S((T, D), BF)] * 3 + [S((T, 128), BF)] + [S((T, D), BF)] * 3,
+        scratch_shapes=[pltpu.VMEM((T, D), BF), pltpu.VMEM((NP, T, 128), BF), pltpu.VMEM((NP, T, 128), BF),
                         pltpu.VMEM((per, 2, L, 128), F32), pltpu.VMEM((per, 2, L, 128), F32), sem, sem, sem, sem],
         compiler_params=pltpu.CompilerParams(collective_id=collective_id, has_side_effects=True, vmem_limit_bytes=60 << 20),
-        name="att_fwd")(q, k, v, e, bt, qseg, kseg, k, v)
+        name="att_fwd")(feat, w, vec, e, bt, qseg, kseg)
 
 
 def widen_kernel(*refs):
@@ -491,7 +503,7 @@
     return pl.pallas_call(
         widen_kernel, grid=(parts,), in_specs=[spec(a) for a in arrays], out_specs=[spec(a) for a in arrays],
         out_shape=[jax.ShapeDtypeStruct(a.shape, F32) for a in arrays],
-        compiler_params=pltpu.CompilerParams(vmem_limit_bytes=32 << 20), name="widen")(*arrays)
+        compiler_params=pltpu.CompilerParams(vmem_limit_bytes=62 << 20), name="widen")(*arrays)
 
 
 def gelu_both(u):
@@ -642,16 +654,13 @@
     norm_gains, norm_shifts = ln_gain[0], ln_shift[0]
     bias_rows = attn_bias[0]
     qkv_weight, out_weight, up_weight, down_weight = w_qkv[0], w_out[0], w_up[0], w_down[0]
-    plain_in = features[0].reshape(tokens, width).astype(jnp.float32)
-    normed = layer_norm(plain_in, norm_gains[0], norm_shifts[0]).astype(BF)
-    combined = jnp.dot(normed, qkv_weight, preferred_element_type=jnp.float32)
-    queries = (combined[:, :width] + bias_rows[0]).astype(BF) * BF(0.125)
-    key_part = combined[:, width:2 * width].astype(BF)
-    value_part = (combined[:, 2 * width:] + bias_rows[1]).astype(BF)
     e, et, qseg, kseg = prepare(segment_ids, box_cells[0], distance_table[0], is_vision)
     onehot = code_onehot()
     bt = jnp.dot(distance_table[0].T.astype(BF), onehot, preferred_element_type=jnp.float32).astype(BF).reshape(heads, 256, 256)
-    attended, partner_k, partner_v, qmisc = front(queries, key_part, value_part, e, bt, qseg, kseg, length, 6)
+    feat = features[0].reshape(tokens, width)
+    vec_one = jnp.concatenate([norm_gains[0:1], norm_shifts[0:1], bias_rows[0:2], jnp.zeros((4, width), F32)])
+    attended, partner_k, partner_v, qmisc, queries, key_part, value_part = front(
+        feat, qkv_weight, vec_one, e, bt, qseg, kseg, length, 6)
     vec = jnp.concatenate([bias_rows[2:3], norm_gains[1:2], norm_shifts[1:2], down_bias, jnp.zeros((4, width), F32)])
     q_send, m_send = lax.optimization_barrier((queries, qmisc))
     partner_q = from_partner(q_send, "stream", 0)
@@ -663,7 +672,6 @@
     output = output.reshape(1, rows, length, width)
     small_up = grad_up_bias.reshape(-1, 128)
     early = jnp.concatenate([small_mid.reshape(-1, 128), small_up])
-    vec_one = jnp.concatenate([norm_gains[0:1], norm_shifts[0:1], jnp.zeros((6, width), F32)])
     input_grad, small_a, sum_up, sum_down, sum_out, sum_qkv = back(
         queries, key_part, partner_k, value_part, partner_v, grad_attended, dmisc, qmisc, e, et, bt, kseg,
         partner_q, partner_m, features[0].reshape(tokens, width), qkv_weight, grad_middle, vec_one, early,

time: 390 us -> 377 us (0.967); the launches traced: 383 us -> 375 us
  Pallas kernels: 338 us -> 348 us
  local copies, waits for them, and re-layouts: 18.6 us -> 10.7 us
  other arithmetic: 15.8 us -> 9.14 us
    unnamed x46 -> x23, local copies, waits for them, and re-layouts: 12.2 us -> 3.04 us
    pallas_call x1, Pallas kernels: 10.6 us -> 17.4 us  [widen(): pl.pallas_call(widen_kernel, grid=(parts,), in_specs=[spec(a) for a in ar...]
    pallas_call x1, Pallas kernels: 77.8 us -> 82.1 us  [front(): pl.pallas_call(functools.partial(front_kernel, NP, R), grid=(2 * per,), i...]
  transfers between devices with their start and end apart: 2 -> 2, of which waited for: 0 -> 0; matrix products, arithmetic and copies ran while one was open for 1% -> 1% of each run, Pallas kernels for 13% -> 14%
where the time goes in v3:
time: 377 us; the launch traced here: 375 us
  Pallas kernels  348 us (92%)
  local copies, waits for them, and re-layouts  10.7 us (3%)
  other arithmetic  9.14 us (2%)
    pallas_call x1, Pallas kernels, back(): pl.pallas_call(functools.partial(back_kernel, n, NP, R, chunks, loads, cu...  198 us
    pallas_call x1, Pallas kernels, front(): pl.pallas_call(functools.partial(front_kernel, NP, R), grid=(2 * per,), i...  82.1 us
    pallas_call x1, Pallas kernels, mid(): pl.pallas_call(functools.partial(mid_kernel, RC), grid=(FF // FT,), in_sp...  51.2 us
    pallas_call x1, Pallas kernels, widen(): pl.pallas_call(widen_kernel, grid=(parts,), in_specs=[spec(a) for a in ar...  17.4 us
  transfers between devices with their start and end apart: 2, of which 0 were waited for; matrix products, arithmetic and copies ran while one was open for 1% of the time, Pallas kernels for 14%

profile of v3, /device:TPU:0, one launch (start us, length us, event | category | flops | bytes accessed | tf_op | source)
XLA Modules:
  0.0 374.9 jit_solution(1246140681408266028)
XLA Ops:
  0.6 0.2 fusion.15
  0.9 0.7 slice.110
  1.6 0.8 slice_add_fusion
  2.3 1.0 fusion.1.e_ref
  3.4 0.7 convert_element_type.28
  4.0 2.6 convolution_convert_fusion
  6.7 0.5 copy.35
  7.1 0.0 copy-start.3
  7.2 0.0 copy-start.1
  7.2 0.0 copy-start.2
  7.2 1.3 slice.140.b_ref
  8.4 0.0 copy-done.3
  8.4 0.0 copy-done.1
  8.4 0.0 copy-done.2
  8.5 0.9 compare_convert_fusion.qseg_ref
  9.4 0.9 select_convert_fusion.kseg_ref
  10.3 0.6 pad_maximum_fusion.1.vec_ref
  10.9 0.0 copy-start.4
  10.9 82.1 %att_fwd.1 = (bf16[1024,768]{1,0:T(8,128)(2,1)}, bf16[1024,768]{1,0:T(8,128)(2,1)}, bf16[1024,768]{1,0:T(8,128)(2,1)}, bf16[1024,128]{1,0:T(8,128)(2,1)}, bf16[1...) custom-call(bf16[1024,768]{1,0:T(8,128)(2,1)} %bitcast.101, ...), custom_call_target="tpu_custom_call" | custom-call | tf_op jit(solution)/shard_map/att_fwd/pallas_call | solution.py:483
  93.0 0.1 collective-permute-start
  93.1 2.0 collective-permute-start.1
  95.1 0.7 slice_bitcast_fusion.10
  95.8 0.0 copy-done.4
  95.8 0.6 concatenate.14.vec_ref
  96.4 51.2 %feed_forward.1 = (bf16[1024,768]{1,0:T(8,128)(2,1)}, f32[1024,768]{1,0:T(8,128)}, bf16[1024,768]{1,0:T(8,128)(2,1)}, bf16[1024,128]{1,0:T(8,128)(2,1)}, bf16[76...) custom-call(bf16[1024,768]{1,0:T(8,128)(2,1)} %bitcast.102, ...), custom_call_target="tpu_custom_call" | custom-call | tf_op jit(solution)/shard_map/feed_forward/pallas_call | solution.py:590
  147.7 0.7 reshape.187
  148.4 1.3 pad_maximum_fusion.early_ref
  149.7 0.6 add_minimum_fusion
  150.3 0.9 fusion.2.et_ref
  151.2 0.0 collective-permute-done.1.qmf_ref
  151.2 0.0 collective-permute-done.qf_ref
  151.2 197.6 %att_bwd.1 = (bf16[1024,768]{1,0:T(8,128)(2,1)}, f32[288,128]{1,0:T(8,128)}, bf16[768,3072]{1,0:T(8,128)(2,1)}, bf16[3072,768]{1,0:T(8,128)(2,1)}, bf16[768,768]{1,0:T(8,128)(2,1)}, /*index=5*/bf16[768,2304]{1,0:T(8,128)(2,1)}) custom-call(bf16[1024,768]{1,0:T(8,128)(2,1)} %get-tuple-element.50.q_ref, bf16[1024,768]{1,0:T(8,128)(2,1)} %get-tuple-element.43.kn_ref, ...), custom_call_target="tpu_custom_call" | custom-call | tf_op jit(solution)/shard_map/att_bwd/pallas_call | solution.py:346
  348.9 0.8 slice_bitcast_fusion
  349.6 0.9 slice.134
  350.5 1.3 slice.135
  351.9 0.6 broadcast_in_dim.42
  352.5 1.0 convolution_bitcast_fusion
  353.6 0.1 copy.30
  353.7 0.7 reshape.195
  354.4 0.6 copy.61
  355.0 0.6 maximum_bitcast_fusion
  355.6 0.6 maximum_bitcast_fusion.1
  356.2 0.0 copy-start
  356.2 17.4 %widen.1 = (f32[768,2304]{1,0:T(8,128)}, f32[768,768]{1,0:T(8,128)}, f32[768,3072]{1,0:T(8,128)}, f32[3072,768]{1,0:T(8,128)}) custom-call(bf16[768,2304]{1,0:T(8,128)(2,1)} %get-tuple-element.60.refs_0_, bf16[768,768]{1,0:T(8,128)(2,1)} %get-tuple-element.61.refs_1_, bf16[768,3072]{1,0:T(8,128)(2,1)} %get-tuple-element.62.refs_2_, ...), custom_call_target="tpu_custom_call" | custom-call | tf_op jit(solution)/shard_map/widen/pallas_call | solution.py:503
  373.6 0.0 copy-done
  373.6 1.1 copy.70
  (16 shorter events, 0.1 us)
Async XLA Ops:
  7.1 1.3 copy-start.3
  7.2 1.3 copy-start.1
  7.2 1.3 copy-start.2
  10.9 84.9 %copy-start.4 = (f32[1,768]{1,0:T(1,128)S(1)}, f32[1,768]{1,0:T(1,128)}, u32[]{:S(2)}) copy-start(f32[1,768]{1,0:T(1,128)} %param.27) | copy-start | bytes 9220
  93.0 58.2 %collective-permute-start = (bf16[1024,768]{1,0:T(8,128)(2,1)}, bf16[1024,768]{1,0:T(8,128)(2,1)}, u32[]{:S(2)}, u32[]{:S(2)}) collective-permute-start(bf16[1024,768]{1,0:T(8,128)(2,1)} %get-tuple-element.50.q_ref), channel_id=1, source_target_pairs={{0,16},{16,0},{1,17},{17,1},{2,18},{18,2},{3,19},{19,3},{4,20},{20... | collective-permute-start | bytes 4718600 | tf_op jit(solution)/shard_map/ppermute | solution.py:605
  93.1 58.1 %collective-permute-start.1 = (bf16[1024,128]{1,0:T(8,128)(2,1)}, bf16[1024,128]{1,0:T(8,128)(2,1)}, u32[]{:S(2)}, u32[]{:S(2)}) collective-permute-start(bf16[1024,128]{1,0:T(8,128)(2,1)} %get-tuple-element.51.qm_ref), channel_id=1, source_target_pairs={{0,16},{16,0},{1,17},{17,1},{2,18},{18,2},{3,19},{19,3},{4,20},{20... | collective-permute-start | bytes 786440 | tf_op jit(solution)/shard_map/ppermute | solution.py:605
  356.2 17.4 %copy-start = (bf16[1024,768]{1,0:T(8,128)(2,1)S(1)}, bf16[1024,768]{1,0:T(8,128)(2,1)}, u32[]{:S(2)}) copy-start(bf16[1024,768]{1,0:T(8,128)(2,1)} %get-tuple-element.58) | copy-start | bytes 4718596
